TPU v7x, 128 devices: a whole 4x4x4 slice. The times are simulated.
128 devices in a mesh: chan: 8 (over y_lo, x), seq: 16 (over y_hi, z, core).
Axes of the slice: x: 4, y: 4 (y_hi: 2, y_lo: 2; y = y_hi * 2 + y_lo), z: 4, core: 2. Of those that a mesh axis runs over, the one named last changes fastest.
Arguments:
- projected: bfloat16 [3, 32768, 4096], P(None, ('chan', 'seq')), may hold values from -6 to 6
- short_filter: float32 [3, 3, 4096], replicated, may hold values from -3 to 3
- residues: float32 [16, 4096], P(None, ('chan', 'seq')), may hold values from -3 to 3
- decays: float32 [16, 4096], P(None, ('chan', 'seq')), may hold values from 1.5258789e-05 to 0.04
- skip: float32 [4096], P(('chan', 'seq')), may hold values from -4 to 4
Outputs:
- mixed: bfloat16 [32768, 4096], P(('chan', 'seq'))
All inputs are finite; a program needn't handle non-finite values.
Results may differ from a plain program's by a relative error of at most 0.01055.
Values may be sent and summed in bfloat16 or wider, within the bound.
A program may use at most 320 MiB of HBM per device.

v0:
```python
import math

import jax
import jax.numpy as jnp
from jax import lax
from jax.sharding import PartitionSpec as P


def passed_along(value, axis, steps):
    count = lax.axis_size(axis)
    first, last = (max(0, -steps), min(count, count - steps))
    return lax.ppermute(value, axis, [(source, source + steps) for source in range(first, last)])


def angle_table(row_count, col_count, period):
    product = lax.broadcasted_iota(jnp.int32, (row_count, col_count), 0) * lax.broadcasted_iota(
        jnp.int32, (row_count, col_count), 1
    )
    return (product % period).astype(jnp.float32) * (2.0 * math.pi / period)


def convolve(owned, residues, decays, skip):
    channels, length = owned.shape
    n_total = 2 * length
    n_one = 1 << (n_total.bit_length() - 1) // 2
    n_two = n_total // n_one
    half_one = n_one // 2
    precise = lax.Precision.HIGH
    signal = owned.astype(jnp.float32)
    folded = signal.reshape(channels, half_one, n_two)
    first = angle_table(n_one, half_one, n_one)
    cos_one = jnp.cos(first)
    sin_one = jnp.sin(first)
    twist = angle_table(n_one, n_two, n_total)
    twist_cos = jnp.cos(twist)
    twist_sin = jnp.sin(twist)
    second = angle_table(n_two, n_two, n_two)
    cos_two = jnp.cos(second)
    sin_two = jnp.sin(second)
    section_real = jnp.einsum("kn,cnm->ckm", cos_one, folded, precision=precise)
    section_imag = -jnp.einsum("kn,cnm->ckm", sin_one, folded, precision=precise)
    turned_real = section_real * twist_cos + section_imag * twist_sin
    turned_imag = section_imag * twist_cos - section_real * twist_sin
    freq_real = jnp.einsum("ckm,mj->ckj", turned_real, cos_two, precision=precise) + jnp.einsum(
        "ckm,mj->ckj", turned_imag, sin_two, precision=precise
    )
    freq_imag = jnp.einsum("ckm,mj->ckj", turned_imag, cos_two, precision=precise) - jnp.einsum(
        "ckm,mj->ckj", turned_real, sin_two, precision=precise
    )
    low_index = lax.broadcasted_iota(jnp.int32, (n_one, n_two), 0)
    high_index = lax.broadcasted_iota(jnp.int32, (n_one, n_two), 1)
    frequency = (low_index + n_one * high_index).astype(jnp.float32)
    sine_full = jnp.sin(frequency * (2.0 * math.pi / n_total))
    half_square = 2.0 * jnp.sin(frequency * (math.pi / n_total)) ** 2
    parity = (1 - 2 * (low_index % 2)).astype(jnp.float32)

    def add_mode(mode_index, totals):
        spec_real, spec_imag = totals
        mode_rate = lax.dynamic_index_in_dim(decays, mode_index, 0, keepdims=False)[:, None, None]
        amplitude = lax.dynamic_index_in_dim(residues, mode_index, 0, keepdims=False)[
            :, None, None
        ] * jnp.sqrt(mode_rate)
        factor = jnp.exp(-mode_rate)
        factor_end = jnp.exp(-mode_rate * length)
        denom_real = -jnp.expm1(-mode_rate) + factor * half_square
        denom_imag = factor * sine_full
        scaled = (
            amplitude
            * (1.0 - parity * factor_end)
            / (denom_real * denom_real + denom_imag * denom_imag)
        )
        return (spec_real + scaled * denom_real, spec_imag - scaled * denom_imag)

    zeros = jnp.zeros((channels, n_one, n_two), jnp.float32)
    filter_real, filter_imag = lax.fori_loop(0, decays.shape[0], add_mode, (zeros, zeros))
    prod_real = freq_real * filter_real - freq_imag * filter_imag
    prod_imag = freq_real * filter_imag + freq_imag * filter_real
    back_real = jnp.einsum("ckj,jm->ckm", prod_real, cos_two, precision=precise) - jnp.einsum(
        "ckj,jm->ckm", prod_imag, sin_two, precision=precise
    )
    back_imag = jnp.einsum("ckj,jm->ckm", prod_imag, cos_two, precision=precise) + jnp.einsum(
        "ckj,jm->ckm", prod_real, sin_two, precision=precise
    )
    untwist_real = back_real * twist_cos - back_imag * twist_sin
    untwist_imag = back_imag * twist_cos + back_real * twist_sin
    result = jnp.einsum("kn,ckm->cnm", cos_one, untwist_real, precision=precise) - jnp.einsum(
        "kn,ckm->cnm", sin_one, untwist_imag, precision=precise
    )
    conv = result.reshape(channels, length) / n_total + skip[:, None] * signal
    return conv.astype(jnp.bfloat16)


def shards(projected, short_filter, residues, decays, skip):
    last_rows = projected[:, -2:, :]
    before_rows = passed_along(last_rows, ("chan", "seq"), 1)
    extended = jnp.concatenate([before_rows, projected], axis=1).astype(jnp.float32)
    featured = (
        short_filter[:, 0, None, :] * extended[:, 2:]
        + short_filter[:, 1, None, :] * extended[:, 1:-1]
        + short_filter[:, 2, None, :] * extended[:, :-2]
    )
    gated = (featured[1] * featured[2]).astype(jnp.bfloat16)
    by_channel = gated.T
    owned = lax.all_to_all(by_channel, ("chan", "seq"), split_axis=0, concat_axis=1, tiled=True)
    conv = convolve(owned, residues, decays, skip)
    returned = lax.all_to_all(conv, ("chan", "seq"), split_axis=1, concat_axis=0, tiled=True)
    token_major = returned.T
    return (featured[0] * token_major.astype(jnp.float32)).astype(jnp.bfloat16)


def solution(mesh):
    return jax.shard_map(
        shards,
        mesh=mesh,
        in_specs=(
            P(None, ("chan", "seq"), None),
            P(),
            P(None, ("chan", "seq")),
            P(None, ("chan", "seq")),
            P(("chan", "seq")),
        ),
        out_specs=P(("chan", "seq"), None),
        check_vma=False,
    )
```

profile of v0, /device:TPU:1, one launch (start us, length us, event | category | flops | bytes accessed | tf_op | source)
XLA Modules:
  0.0 483.0 jit_solution(15892050265041315279)
XLA Ops:
  1.0 4.9 %collective-permute-start = (bf16[3,2,4096]{2,1,0:T(2,128)(2,1)S(1)}, bf16[3,2,4096]{2,1,0:T(2,128)(2,1)S(1)}, u32[]{:S(2)}, u32[]{:S(2)}) collective-permute-start(bf16[3,2,4096]{2,1,0:T(2,128)(2,1)S(1)} %slice.31), channel_id=1, source_target_pairs={{0,1},{1,2},{2,3},{3,4},{4,5},{5,6},{6,7},{7,8},{8,9},{9,10},{10,1... | collective-permute-start | bytes 147464 | tf_op jit(solution)/shard_map/ppermute | solution.py:12
  7.3 8.6 %copy.32 = bf16[3,256,4096]{1,2,0:T(8,128)(2,1)} copy(bf16[3,256,4096]{2,1,0:T(8,128)(2,1)} %param.7) | data formatting | bytes 12582912 | tf_op args[0]
  17.5 13.0 %maximum_convert_fusion = f32[3,258,4096]{1,2,0:T(8,128)} fusion(bf16[3,256,4096]{1,2,0:T(8,128)(2,1)} %copy.32, bf16[3,2,4096]{1,2,0:T(8,128)(2,1)S(1)} %copy.31), kind=kLoop, calls=%fused_computation.25 | loop fusion | flops 12681216 | bytes 19021824 | tf_op jit(solution)/shard_map/convert_element_type | solution.py:96
  30.5 18.2 %fusion.10 = f32[3,256,4096]{1,2,0:T(8,128)S(1)} fusion(f32[3,258,4096]{1,2,0:T(8,128)} %maximum_convert_fusion, f32[3,4096]{1,0:T(4,128)S(1)} %get-tuple-element.270, f32[3,4096]{1,0:T(4,128)S(1)} %get-tuple-element.271, f32[3,4096]{1,0:T(4,128)S(1)} %bitcast.106), kind=kLoop, calls=%fused_computation.21 | loop fusion | flops 15728640 | bytes 50479104 | tf_op jit(solution)/shard_map/add | solution.py:98
  48.8 4.5 copy-done.4
  53.3 1.8 fusion.22
  55.2 10.5 %all-to-all-start = ((bf16[128,32,256]{2,1,0:T(8,128)(2,1)}), bf16[128,32,256]{2,1,0:T(8,128)(2,1)}, u32[]{:S(2)}, u32[]{:S(2)}) async-start(bf16[128,32,256]{2,1,0:T(8,128)(2,1)} %bitcast.3), calls=%async_computation | async-start | bytes 4194304 | tf_op jit(solution)/shard_map/all_to_all | solution.py:104
  65.6 232.1 %while.18 = (s32[]{:T(128)}, f32[32,256,256]{2,1,0:T(8,128)}, f32[32,256,256]{2,1,0:T(8,128)}, f32[16,32]{1,0:T(8,128)}, f32[16,32]{1,0:T(8,128)}, /*index=5*/s3...) while((s32[]{:T(128)}, f32[32,256,256]{2,1,0:T(8,128)}, ...), condition=%wide.region_1.2_spmd.clone.clone.clone, body=%wide.region_0.1_spmd.clone.clone.clone.sunk | while | flops 34209920 | bytes 35132032 | solution.py:75
  66.6 1.7 multiply_sine_fusion.2
  68.3 8.7 %fusion.154 = (f32[32,256,256]{2,1,0:T(8,128)}, f32[32,256,256]{2,1,0:T(8,128)}) fusion(f32[32,256,256]{2,1,0:T(8,128)} %get-tuple-element.358, f32[256,256]{1,0:T(8,128)S(1)} %get-tuple-element.337, f32[32]{0:T(128)S(1)} %get-tuple-element.338, f32[256,256]{1,0:T(8,128)S(1)} %get-tuple-element.339, f32[32]{0:T(128)S(1)} %get-tuple-element.340, ...), kind=kLoop, calls=%fused_computation.7.clone.1 | loop fusion | flops 33554432 | bytes 34341376 | tf_op jit(solution)/shard_map/while/body/eval_jaxpr/sub | solution.py:72
  79.6 12.1 %fusion.154 = (f32[32,256,256]{2,1,0:T(8,128)}, f32[32,256,256]{2,1,0:T(8,128)}) fusion(f32[32,256,256]{2,1,0:T(8,128)} %get-tuple-element.358, f32[256,256]{1,0:T(8,128)S(1)} %get-tuple-element.337, f32[32]{0:T(128)S(1)} %get-tuple-element.338, f32[256,256]{1,0:T(8,128)S(1)} %get-tuple-element.339, f32[32]{0:T(128)S(1)} %get-tuple-element.340, ...), kind=kLoop, calls=%fused_computation.7.clone.1 | loop fusion | flops 33554432 | bytes 34341376 | tf_op jit(solution)/shard_map/while/body/eval_jaxpr/sub | solution.py:72
  92.6 1.7 multiply_sine_fusion.2
  94.3 12.1 %fusion.154 = (f32[32,256,256]{2,1,0:T(8,128)}, f32[32,256,256]{2,1,0:T(8,128)}) fusion(f32[32,256,256]{2,1,0:T(8,128)} %get-tuple-element.358, f32[256,256]{1,0:T(8,128)S(1)} %get-tuple-element.337, f32[32]{0:T(128)S(1)} %get-tuple-element.338, f32[256,256]{1,0:T(8,128)S(1)} %get-tuple-element.339, f32[32]{0:T(128)S(1)} %get-tuple-element.340, ...), kind=kLoop, calls=%fused_computation.7.clone.1 | loop fusion | flops 33554432 | bytes 34341376 | tf_op jit(solution)/shard_map/while/body/eval_jaxpr/sub | solution.py:72
  107.3 1.7 multiply_sine_fusion.2
  109.0 12.1 %fusion.154 = (f32[32,256,256]{2,1,0:T(8,128)}, f32[32,256,256]{2,1,0:T(8,128)}) fusion(f32[32,256,256]{2,1,0:T(8,128)} %get-tuple-element.358, f32[256,256]{1,0:T(8,128)S(1)} %get-tuple-element.337, f32[32]{0:T(128)S(1)} %get-tuple-element.338, f32[256,256]{1,0:T(8,128)S(1)} %get-tuple-element.339, f32[32]{0:T(128)S(1)} %get-tuple-element.340, ...), kind=kLoop, calls=%fused_computation.7.clone.1 | loop fusion | flops 33554432 | bytes 34341376 | tf_op jit(solution)/shard_map/while/body/eval_jaxpr/sub | solution.py:72
  122.0 1.7 multiply_sine_fusion.2
  123.8 12.1 %fusion.154 = (f32[32,256,256]{2,1,0:T(8,128)}, f32[32,256,256]{2,1,0:T(8,128)}) fusion(f32[32,256,256]{2,1,0:T(8,128)} %get-tuple-element.358, f32[256,256]{1,0:T(8,128)S(1)} %get-tuple-element.337, f32[32]{0:T(128)S(1)} %get-tuple-element.338, f32[256,256]{1,0:T(8,128)S(1)} %get-tuple-element.339, f32[32]{0:T(128)S(1)} %get-tuple-element.340, ...), kind=kLoop, calls=%fused_computation.7.clone.1 | loop fusion | flops 33554432 | bytes 34341376 | tf_op jit(solution)/shard_map/while/body/eval_jaxpr/sub | solution.py:72
  138.5 12.1 %fusion.154 = (f32[32,256,256]{2,1,0:T(8,128)}, f32[32,256,256]{2,1,0:T(8,128)}) fusion(f32[32,256,256]{2,1,0:T(8,128)} %get-tuple-element.358, f32[256,256]{1,0:T(8,128)S(1)} %get-tuple-element.337, f32[32]{0:T(128)S(1)} %get-tuple-element.338, f32[256,256]{1,0:T(8,128)S(1)} %get-tuple-element.339, f32[32]{0:T(128)S(1)} %get-tuple-element.340, ...), kind=kLoop, calls=%fused_computation.7.clone.1 | loop fusion | flops 33554432 | bytes 34341376 | tf_op jit(solution)/shard_map/while/body/eval_jaxpr/sub | solution.py:72
  151.5 1.7 multiply_sine_fusion.2
  153.2 12.1 %fusion.154 = (f32[32,256,256]{2,1,0:T(8,128)}, f32[32,256,256]{2,1,0:T(8,128)}) fusion(f32[32,256,256]{2,1,0:T(8,128)} %get-tuple-element.358, f32[256,256]{1,0:T(8,128)S(1)} %get-tuple-element.337, f32[32]{0:T(128)S(1)} %get-tuple-element.338, f32[256,256]{1,0:T(8,128)S(1)} %get-tuple-element.339, f32[32]{0:T(128)S(1)} %get-tuple-element.340, ...), kind=kLoop, calls=%fused_computation.7.clone.1 | loop fusion | flops 33554432 | bytes 34341376 | tf_op jit(solution)/shard_map/while/body/eval_jaxpr/sub | solution.py:72
  166.2 1.7 multiply_sine_fusion.2
  167.9 12.1 %fusion.154 = (f32[32,256,256]{2,1,0:T(8,128)}, f32[32,256,256]{2,1,0:T(8,128)}) fusion(f32[32,256,256]{2,1,0:T(8,128)} %get-tuple-element.358, f32[256,256]{1,0:T(8,128)S(1)} %get-tuple-element.337, f32[32]{0:T(128)S(1)} %get-tuple-element.338, f32[256,256]{1,0:T(8,128)S(1)} %get-tuple-element.339, f32[32]{0:T(128)S(1)} %get-tuple-element.340, ...), kind=kLoop, calls=%fused_computation.7.clone.1 | loop fusion | flops 33554432 | bytes 34341376 | tf_op jit(solution)/shard_map/while/body/eval_jaxpr/sub | solution.py:72
  180.9 1.7 multiply_sine_fusion.2
  182.6 12.1 %fusion.154 = (f32[32,256,256]{2,1,0:T(8,128)}, f32[32,256,256]{2,1,0:T(8,128)}) fusion(f32[32,256,256]{2,1,0:T(8,128)} %get-tuple-element.358, f32[256,256]{1,0:T(8,128)S(1)} %get-tuple-element.337, f32[32]{0:T(128)S(1)} %get-tuple-element.338, f32[256,256]{1,0:T(8,128)S(1)} %get-tuple-element.339, f32[32]{0:T(128)S(1)} %get-tuple-element.340, ...), kind=kLoop, calls=%fused_computation.7.clone.1 | loop fusion | flops 33554432 | bytes 34341376 | tf_op jit(solution)/shard_map/while/body/eval_jaxpr/sub | solution.py:72
  197.3 12.1 %fusion.154 = (f32[32,256,256]{2,1,0:T(8,128)}, f32[32,256,256]{2,1,0:T(8,128)}) fusion(f32[32,256,256]{2,1,0:T(8,128)} %get-tuple-element.358, f32[256,256]{1,0:T(8,128)S(1)} %get-tuple-element.337, f32[32]{0:T(128)S(1)} %get-tuple-element.338, f32[256,256]{1,0:T(8,128)S(1)} %get-tuple-element.339, f32[32]{0:T(128)S(1)} %get-tuple-element.340, ...), kind=kLoop, calls=%fused_computation.7.clone.1 | loop fusion | flops 33554432 | bytes 34341376 | tf_op jit(solution)/shard_map/while/body/eval_jaxpr/sub | solution.py:72
  212.1 12.1 %fusion.154 = (f32[32,256,256]{2,1,0:T(8,128)}, f32[32,256,256]{2,1,0:T(8,128)}) fusion(f32[32,256,256]{2,1,0:T(8,128)} %get-tuple-element.358, f32[256,256]{1,0:T(8,128)S(1)} %get-tuple-element.337, f32[32]{0:T(128)S(1)} %get-tuple-element.338, f32[256,256]{1,0:T(8,128)S(1)} %get-tuple-element.339, f32[32]{0:T(128)S(1)} %get-tuple-element.340, ...), kind=kLoop, calls=%fused_computation.7.clone.1 | loop fusion | flops 33554432 | bytes 34341376 | tf_op jit(solution)/shard_map/while/body/eval_jaxpr/sub | solution.py:72
  226.8 12.1 %fusion.154 = (f32[32,256,256]{2,1,0:T(8,128)}, f32[32,256,256]{2,1,0:T(8,128)}) fusion(f32[32,256,256]{2,1,0:T(8,128)} %get-tuple-element.358, f32[256,256]{1,0:T(8,128)S(1)} %get-tuple-element.337, f32[32]{0:T(128)S(1)} %get-tuple-element.338, f32[256,256]{1,0:T(8,128)S(1)} %get-tuple-element.339, f32[32]{0:T(128)S(1)} %get-tuple-element.340, ...), kind=kLoop, calls=%fused_computation.7.clone.1 | loop fusion | flops 33554432 | bytes 34341376 | tf_op jit(solution)/shard_map/while/body/eval_jaxpr/sub | solution.py:72
  241.5 12.1 %fusion.154 = (f32[32,256,256]{2,1,0:T(8,128)}, f32[32,256,256]{2,1,0:T(8,128)}) fusion(f32[32,256,256]{2,1,0:T(8,128)} %get-tuple-element.358, f32[256,256]{1,0:T(8,128)S(1)} %get-tuple-element.337, f32[32]{0:T(128)S(1)} %get-tuple-element.338, f32[256,256]{1,0:T(8,128)S(1)} %get-tuple-element.339, f32[32]{0:T(128)S(1)} %get-tuple-element.340, ...), kind=kLoop, calls=%fused_computation.7.clone.1 | loop fusion | flops 33554432 | bytes 34341376 | tf_op jit(solution)/shard_map/while/body/eval_jaxpr/sub | solution.py:72
  256.2 12.1 %fusion.154 = (f32[32,256,256]{2,1,0:T(8,128)}, f32[32,256,256]{2,1,0:T(8,128)}) fusion(f32[32,256,256]{2,1,0:T(8,128)} %get-tuple-element.358, f32[256,256]{1,0:T(8,128)S(1)} %get-tuple-element.337, f32[32]{0:T(128)S(1)} %get-tuple-element.338, f32[256,256]{1,0:T(8,128)S(1)} %get-tuple-element.339, f32[32]{0:T(128)S(1)} %get-tuple-element.340, ...), kind=kLoop, calls=%fused_computation.7.clone.1 | loop fusion | flops 33554432 | bytes 34341376 | tf_op jit(solution)/shard_map/while/body/eval_jaxpr/sub | solution.py:72
  270.9 12.1 %fusion.154 = (f32[32,256,256]{2,1,0:T(8,128)}, f32[32,256,256]{2,1,0:T(8,128)}) fusion(f32[32,256,256]{2,1,0:T(8,128)} %get-tuple-element.358, f32[256,256]{1,0:T(8,128)S(1)} %get-tuple-element.337, f32[32]{0:T(128)S(1)} %get-tuple-element.338, f32[256,256]{1,0:T(8,128)S(1)} %get-tuple-element.339, f32[32]{0:T(128)S(1)} %get-tuple-element.340, ...), kind=kLoop, calls=%fused_computation.7.clone.1 | loop fusion | flops 33554432 | bytes 34341376 | tf_op jit(solution)/shard_map/while/body/eval_jaxpr/sub | solution.py:72
  285.6 12.1 %fusion.154 = (f32[32,256,256]{2,1,0:T(8,128)}, f32[32,256,256]{2,1,0:T(8,128)}) fusion(f32[32,256,256]{2,1,0:T(8,128)} %get-tuple-element.358, f32[256,256]{1,0:T(8,128)S(1)} %get-tuple-element.337, f32[32]{0:T(128)S(1)} %get-tuple-element.338, f32[256,256]{1,0:T(8,128)S(1)} %get-tuple-element.339, f32[32]{0:T(128)S(1)} %get-tuple-element.340, ...), kind=kLoop, calls=%fused_computation.7.clone.1 | loop fusion | flops 33554432 | bytes 34341376 | tf_op jit(solution)/shard_map/while/body/eval_jaxpr/sub | solution.py:72
  299.9 3.7 copy.33
  303.6 2.8 fusion.34
  306.5 2.8 fusion.36
  309.3 10.8 %fusion.42 = f32[32,256,256]{2,1,0:T(8,128)} fusion(f32[32,256,256]{2,1,0:T(8,128)S(1)} %fusion.36, f32[32,256,256]{2,1,0:T(8,128)S(1)} %fusion.34, f32[256,256]{0,1:T(8,128)S(1)} %copy.35, f32[256,256]{0,1:T(8,128)S(1)} %copy.34), kind=kOutput, calls=%fused_computation.63 | convolution fusion | flops 3230531584 | bytes 25690112 | tf_op jit(solution)/shard_map/ckm,mj->ckj/dot_general | solution.py:47
  320.1 11.2 %fusion.40 = f32[32,256,256]{2,1,0:T(8,128)} fusion(f32[32,256,256]{2,1,0:T(8,128)S(1)} %fusion.36, f32[32,256,256]{2,1,0:T(8,128)S(1)} %fusion.34, f32[256,256]{0,1:T(8,128)S(1)} %copy.35, f32[256,256]{0,1:T(8,128)S(1)} %copy.34), kind=kOutput, calls=%fused_computation.62 | convolution fusion | flops 3230531584 | bytes 25690112 | tf_op jit(solution)/shard_map/ckm,mj->ckj/dot_general | solution.py:44
  331.3 10.8 %fusion.44 = f32[32,256,256]{2,1,0:T(8,128)} fusion(f32[32,256,256]{2,1,0:T(8,128)S(1)} %fusion.36, f32[32,256,256]{2,1,0:T(8,128)S(1)} %fusion.34, f32[256,256]{0,1:T(8,128)S(1)} %copy.35, f32[256,256]{0,1:T(8,128)S(1)} %copy.34), kind=kOutput, calls=%fused_computation.64 | convolution fusion | flops 3230531584 | bytes 25690112 | tf_op jit(solution)/shard_map/ckm,mj->ckj/dot_general | solution.py:44
  342.0 27.5 %multiply_subtract_fusion = (f32[32,256,256]{2,1,0:T(8,128)}, f32[32,256,256]{2,1,0:T(8,128)}) fusion(f32[32,256,256]{2,1,0:T(8,128)} %get-tuple-element.146, f32[32,256,256]{2,1,0:T(8,128)} %get-tuple-element.145, f32[32,256,256]{2,1,0:T(8,128)} %fusion.42, f32[32,256,256]{2,1,0:T(8,128)} %fusion.44, f32[32,256,256]{2,1,0:T(8,128)} %fusion.40, ...), kind=kOutput, calls=%fused_computation.41 | convolution fusion | flops 3247308800 | bytes 76021760 | tf_op jit(solution)/shard_map/ckm,mj->ckj/dot_general | solution.py:47
  369.5 8.9 %fusion.52 = f32[32,256,256]{1,2,0:T(8,128)S(1)} fusion(f32[32,256,256]{2,1,0:T(8,128)} %get-tuple-element.265), kind=kOutput, calls=%fused_computation.74 | convolution fusion | flops 3222142976 | bytes 16777216 | tf_op jit(solution)/shard_map/ckj,jm->ckm/dot_general | solution.py:81
  378.5 7.6 %fusion.60 = f32[32,256,256]{1,2,0:T(8,128)} fusion(f32[32,256,256]{2,1,0:T(8,128)S(1)} %copy-done.2), kind=kOutput, calls=%fused_computation.82 | convolution fusion | flops 3222142976 | bytes 16777216 | tf_op jit(solution)/shard_map/ckj,jm->ckm/dot_general | solution.py:78
  386.1 8.0 %fusion.58 = f32[32,256,256]{1,2,0:T(8,128)} fusion(f32[32,256,256]{2,1,0:T(8,128)S(1)} %bitcast.105), kind=kOutput, calls=%fused_computation.80 | convolution fusion | flops 3222142976 | bytes 16777216 | tf_op jit(solution)/shard_map/ckj,jm->ckm/dot_general | solution.py:81
  394.1 7.6 %fusion.54 = f32[32,256,256]{1,2,0:T(8,128)} fusion(f32[32,256,256]{2,1,0:T(8,128)S(1)} %bitcast.105), kind=kOutput, calls=%fused_computation.76 | convolution fusion | flops 3222142976 | bytes 16777216 | tf_op jit(solution)/shard_map/ckj,jm->ckm/dot_general | solution.py:78
  401.7 15.5 %fusion.14 = f32[32,256,128]{2,1,0:T(8,128)} fusion(f32[256,256]{0,1:T(8,128)S(1)} %copy.35, f32[256,256]{0,1:T(8,128)S(1)} %copy.34, f32[32,256,256]{1,2,0:T(8,128)} %fusion.58, f32[32,256,256]{1,2,0:T(8,128)S(1)} %fusion.52, f32[32,256,256]{1,2,0:T(8,128)} %fusion.60, f32[32,256,256]{1,2,0:T(8,128)} %fusion.54), kind=kOutput, calls=%fused_computation.32 | convolution fusion | flops 1621557248 | bytes 38273024 | tf_op jit(solution)/shard_map/kn,ckm->cnm/dot_general | solution.py:86
  417.2 17.2 %fusion.25 = bf16[32,128,256]{1,2,0:T(8,128)(2,1)S(1)} fusion(f32[32,256,128]{2,1,0:T(8,128)} %fusion.14, bf16[128,32,256]{0,2,1:T(8,128)(2,1)} %copy-done.5, f32[32]{0:T(128)S(1)} %copy-done.6, f32[256,256]{0,1:T(8,128)S(1)} %copy.35, f32[256,256]{0,1:T(8,128)S(1)} %copy.34, f32[32,256,256]{1,2,0:T(8,128)} %fusion.58, f32[32,256,256]{1,2,0:T(8,128)} %copy-done.3, ...), kind=kOutput, calls=%fused_computation.48 | convolution fusion | flops 1627848704 | bytes 42467456 | tf_op jit(solution)/shard_map/kn,ckm->cnm/dot_general | solution.py:86
  434.4 2.9 copy.44
  437.3 39.9 %all_to_all.26 = bf16[32,128,256]{2,0,1:T(8,128)(2,1)S(1)} all-to-all(bf16[32,128,256]{2,0,1:T(8,128)(2,1)} %copy.44), channel_id=1, replica_groups=mesh['chan'=8,'seq'=16] {'chan','seq'}, dimensions={1} | all-to-all | bytes 4194304 | tf_op jit(solution)/shard_map/all_to_all | solution.py:106
  477.2 2.8 fusion.24
  480.0 2.9 copy.45
  (75 shorter events, 36.2 us)
Async XLA Ops:
  1.0 15.0 %collective-permute-start = (bf16[3,2,4096]{2,1,0:T(2,128)(2,1)S(1)}, bf16[3,2,4096]{2,1,0:T(2,128)(2,1)S(1)}, u32[]{:S(2)}, u32[]{:S(2)}) collective-permute-start(bf16[3,2,4096]{2,1,0:T(2,128)(2,1)S(1)} %slice.31), channel_id=1, source_target_pairs={{0,1},{1,2},{2,3},{3,4},{4,5},{5,6},{6,7},{7,8},{8,9},{9,10},{10,1... | collective-permute-start | bytes 147464 | tf_op jit(solution)/shard_map/ppermute | solution.py:12
  48.8 4.5 copy-start.4
  55.2 244.8 %all-to-all-start = ((bf16[128,32,256]{2,1,0:T(8,128)(2,1)}), bf16[128,32,256]{2,1,0:T(8,128)(2,1)}, u32[]{:S(2)}, u32[]{:S(2)}) async-start(bf16[128,32,256]{2,1,0:T(8,128)(2,1)} %bitcast.3), calls=%async_computation | async-start | bytes 4194304 | tf_op jit(solution)/shard_map/all_to_all | solution.py:104
  303.6 5.7 %copy-start.5 = (bf16[128,32,256]{0,2,1:T(8,128)(2,1)}, bf16[128,32,256]{0,2,1:T(8,128)(2,1)S(1)}, u32[]{:S(2)}) copy-start(bf16[128,32,256]{0,2,1:T(8,128)(2,1)S(1)} %copy.33) | copy-start | bytes 6291460
  306.5 24.8 %copy-start = (f32[32,256,256]{2,1,0:T(8,128)}, f32[32,256,256]{2,1,0:T(8,128)S(1)}, u32[]{:S(2)}) copy-start(f32[32,256,256]{2,1,0:T(8,128)S(1)} %fusion.34) | copy-start | bytes 25165828
  309.3 22.0 %copy-start.1 = (f32[32,256,256]{2,1,0:T(8,128)}, f32[32,256,256]{2,1,0:T(8,128)S(1)}, u32[]{:S(2)}) copy-start(f32[32,256,256]{2,1,0:T(8,128)S(1)} %fusion.36) | copy-start | bytes 25165828
  369.5 8.9 %copy-start.2 = (f32[32,256,256]{2,1,0:T(8,128)S(1)}, f32[32,256,256]{2,1,0:T(8,128)}, u32[]{:S(2)}) copy-start(f32[32,256,256]{2,1,0:T(8,128)} %get-tuple-element.265) | copy-start | bytes 25165828
  369.5 16.6 %slice-start = ((s8[8388608]{0:T(1024)(128)(4,1)}), s8[4194304]{0:T(1024)(128)(4,1)S(1)}, s32[]{:S(2)}) async-start(s8[8388608]{0:T(1024)(128)(4,1)} %bitcast.104), calls=%async_computation.2 | async-start | bytes 8388608
  378.5 23.3 %copy-start.3 = (f32[32,256,256]{1,2,0:T(8,128)}, f32[32,256,256]{1,2,0:T(8,128)S(1)}, u32[]{:S(2)}) copy-start(f32[32,256,256]{1,2,0:T(8,128)S(1)} %fusion.52) | copy-start | bytes 25165828
  378.5 7.6 %slice-start.1 = ((s8[8388608]{0:T(1024)(128)(4,1)}), s8[4194304]{0:T(1024)(128)(4,1)S(1)}, s32[]{:S(2)}) async-start(s8[8388608]{0:T(1024)(128)(4,1)} %bitcast.104), calls=%async_computation.3 | async-start | bytes 8388608
  401.7 15.5 %copy-start.6 = (f32[32]{0:T(128)S(1)}, f32[32]{0:T(128)}, u32[]{:S(2)}) copy-start(f32[32]{0:T(128)} %param.11) | copy-start | bytes 388
where the time goes:
time: 490 us; the launch traced here: 483 us
  other arithmetic  270 us (55%)
  matrix products  131 us (27%)
  blocking collectives  39.9 us (8%)
  local copies, waits for them, and re-layouts  26.8 us (5%)
  starting transfers between devices  15.4 us (3%)
    sub x16, other arithmetic, add_mode(): return (spec_real + scaled * denom_real, spec_imag - scaled * denom_imag)  190 us
    all_to_all x1, blocking collectives, shards(): lax.all_to_all(conv, ('chan', 'seq'), split_axis=1, concat_axis=0, tiled=...  39.9 us
    sin x16, other arithmetic, convolve(): sine_full = jnp.sin(frequency * (2.0 * math.pi / n_total))  27.6 us
    dot_general x1, matrix products, convolve(): jnp.einsum('ckm,mj->ckj', turned_imag, cos_two, precision=precise)  27.5 us
    add x1, other arithmetic, shards(): short_filter[:, 0, None, :] * extended[:, 2:]  18.2 us
    dot_general x1, matrix products, convolve(): jnp.einsum('kn,ckm->cnm', cos_one, untwist_real, precision=precise)  17.2 us
    dot_general x1, matrix products, convolve(): jnp.einsum('kn,ckm->cnm', sin_one, untwist_imag, precision=precise)  15.5 us
    unnamed x21, local copies, waits for them, and re-layouts  13.3 us
  transfers between devices with their start and end apart: 2, of which 0 were waited for; matrix products, arithmetic and copies ran while one was open for 51% of the time, Pallas kernels for 0%

commit v1 on v0

v1 whole, which is shorter than its diff:
```python
import functools

import jax
import jax.numpy as jnp
from jax import lax
from jax.experimental import pallas as pl
from jax.experimental.pallas import tpu as pltpu
from jax.sharding import PartitionSpec as P

LANES = 128
ROWS = 8
WIDE = LANES * ROWS
BLOCK = 8
PAIR = 16
MESH = pl.DeviceIdType.MESH
F32 = jnp.float32


def token(t):
    return pl.ds((t // ROWS) * ROWS * ROWS + t % ROWS, ROWS, stride=ROWS)


def kernel(
    n_chan,
    n_seq,
    x_hbm,
    filt,
    weight,
    decay,
    skip,
    halo,
    out_hbm,
    xb,
    tiles,
    gated,
    queries,
    ends,
    power,
    power_block,
    taps,
    state,
    got_state,
    before,
    total,
    got_total,
    back,
    carried,
    out_tiles,
    out_rows,
    in_sem,
    out_sem,
    send_state,
    recv_state,
    send_total,
    recv_total,
    send_back,
    recv_back,
):
    groups = gated.shape[0]
    length = x_hbm.shape[1]
    modes = weight.shape[0]
    my_chan = lax.axis_index("chan")
    my_seq = lax.axis_index("seq")

    def fetch(j, m):
        columns = pl.ds(m * WIDE, WIDE)
        return pltpu.make_async_copy(
            x_hbm.at[j, :, columns], xb.at[j, :, columns], in_sem.at[m, j]
        )

    for m in range(groups):
        for j in range(3):
            fetch(j, m).start()

    barrier = pltpu.get_barrier_semaphore()
    for off in range(1, n_seq):
        peer = lax.rem(my_seq + off, n_seq)
        pl.semaphore_signal(barrier, inc=1, device_id=(my_chan, peer), device_id_type=MESH)
    for off in range(1, n_chan):
        peer = lax.rem(my_chan + off, n_chan)
        pl.semaphore_signal(barrier, inc=1, device_id=(peer, my_seq), device_id_type=MESH)

    power[...] = jnp.exp(-decay[...])
    power_block[...] = jnp.exp(-float(BLOCK) * decay[...])

    def feature(m):
        for j in range(3):
            fetch(j, m).wait()
        coefs = [[filt[3 * j + s, m] for s in range(3)] for j in range(3)]

        def step(b, olds):
            for j in range(3):
                rows = xb[j, pl.ds(pl.multiple_of(b * PAIR, PAIR), PAIR), m * WIDE : (m + 1) * WIDE]
                rows = rows.astype(F32)
                for h in range(PAIR // ROWS):
                    for i in range(ROWS):
                        at = (h * ROWS + i) * ROWS
                        tiles[j, at : at + ROWS, :] = rows[
                            h * ROWS : (h + 1) * ROWS, i * LANES : (i + 1) * LANES
                        ]
            olds = list(olds)
            for t in range(PAIR):
                featured = []
                for j in range(3):
                    now = tiles[j, token(t), :]
                    older, old = olds[2 * j], olds[2 * j + 1]
                    featured.append(coefs[j][0] * now + coefs[j][1] * old + coefs[j][2] * older)
                    olds[2 * j], olds[2 * j + 1] = old, now
                place = pl.ds(pl.multiple_of((b * PAIR + t) * ROWS, ROWS), ROWS)
                queries[m, place, :] = featured[0]
                gated[m, place, :] = featured[1] * featured[2]
            return tuple(olds)

        lax.fori_loop(0, length // PAIR, step, tuple(halo[i, m] for i in range(6)))

    def gather_states(m):
        def step(b, states):
            values = [
                gated[m, pl.ds(pl.multiple_of((b * BLOCK + i) * ROWS, ROWS), ROWS), :]
                for i in range(BLOCK)
            ]
            results = []
            for n in range(modes):
                rate = power[n, m]
                end = values[0]
                for i in range(1, BLOCK):
                    end = rate * end + values[i]
                end = weight[n, m] * end
                ends[m, b, n] = end
                results.append(power_block[n, m] * states[n] + end)
            return tuple(results)

        zero = jnp.zeros((ROWS, LANES), F32)
        states = lax.fori_loop(0, length // BLOCK, step, (zero,) * modes)
        for n in range(modes):
            state[m, n] = states[n]

    def state_copy(m, off):
        peer = lax.rem(my_seq + off, n_seq)
        return pltpu.make_async_remote_copy(
            src_ref=state.at[m, peer],
            dst_ref=got_state.at[m, my_seq],
            send_sem=send_state.at[m],
            recv_sem=recv_state.at[m],
            device_id=(my_chan, peer),
            device_id_type=MESH,
        )

    def total_copy(m, off):
        peer = lax.rem(my_chan + off, n_chan)
        return pltpu.make_async_remote_copy(
            src_ref=total.at[m],
            dst_ref=got_total.at[m, my_chan],
            send_sem=send_total.at[m],
            recv_sem=recv_total.at[m],
            device_id=(peer, my_seq),
            device_id_type=MESH,
        )

    def back_copy(m, off):
        peer = lax.rem(my_seq + off, n_seq)
        return pltpu.make_async_remote_copy(
            src_ref=back.at[m, peer],
            dst_ref=carried.at[m, my_seq],
            send_sem=send_back.at[m],
            recv_sem=recv_back.at[m],
            device_id=(my_chan, peer),
            device_id_type=MESH,
        )

    def wait_bytes(ref, count, m, sem):
        some = ref.at[m, pl.ds(0, count)]
        pltpu.make_async_copy(some, some, sem.at[m]).wait()

    def send_states(m):
        for off in range(1, n_seq):
            state_copy(m, off).start()
        got_state[m, my_seq] = state[m, my_seq]

    def scan_group(m):
        wait_bytes(got_state, n_seq - 1, m, recv_state)
        shrink = jnp.exp(-float(length) * decay[my_seq, m])
        running = jnp.zeros((ROWS, LANES), F32)
        for k in range(n_seq):
            before[m, k] = running
            running = shrink * running + got_state[m, k]
        total[m] = running
        for off in range(1, n_chan):
            total_copy(m, off).start()

    def scan_all(m):
        wait_bytes(got_total, n_chan - 1, m, recv_total)
        rate = decay[my_seq, m]
        shrink = jnp.exp(-float(length) * rate)
        shrink_group = jnp.exp(-float(length * n_seq) * rate)
        running = jnp.zeros((ROWS, LANES), F32)
        for c in range(n_chan - 1):
            running = jnp.where(c < my_chan, shrink_group * running + got_total[m, c], running)
        for k in range(n_seq):
            back[m, k] = before[m, k] + running
            running = shrink * running
        for off in range(1, n_seq):
            back_copy(m, off).start()
        carried[m, my_seq] = back[m, my_seq]

    def write(m):
        columns = pl.ds(m * WIDE, WIDE)
        return pltpu.make_async_copy(out_rows.at[:, columns], out_hbm.at[:, columns], out_sem.at[m])

    def convolve(m):
        wait_bytes(carried, n_seq - 1, m, recv_back)
        term = [weight[n, m] for n in range(modes)]
        for i in range(BLOCK):
            tap = term[0]
            for n in range(1, modes):
                tap = tap + term[n]
            taps[i] = tap + skip[m] if i == 0 else tap
            if i < BLOCK - 1:
                term = [term[n] * power[n, m] for n in range(modes)]

        def step(pair, states):
            for half in range(PAIR // BLOCK):
                b = pair * (PAIR // BLOCK) + half
                places = [
                    pl.ds(pl.multiple_of((b * BLOCK + i) * ROWS, ROWS), ROWS) for i in range(BLOCK)
                ]
                values = [gated[m, places[i], :] for i in range(BLOCK)]
                sums = []
                for i in range(BLOCK):
                    one = taps[0] * values[i]
                    for j in range(1, i + 1):
                        one = one + taps[j] * values[i - j]
                    sums.append(one)
                results = []
                for n in range(modes):
                    rate = power[n, m]
                    now = states[n]
                    for i in range(BLOCK):
                        now = now * rate
                        sums[i] = sums[i] + now
                    results.append(now + ends[m, b, n])
                states = tuple(results)
                for i in range(BLOCK):
                    out_tiles[token(half * BLOCK + i), :] = sums[i] * queries[m, places[i], :]
            for i in range(ROWS):
                parts = [
                    out_tiles[(h * ROWS + i) * ROWS : (h * ROWS + i + 1) * ROWS, :]
                    for h in range(PAIR // ROWS)
                ]
                lanes = m * WIDE + i * LANES
                out_rows[pl.ds(pl.multiple_of(pair * PAIR, PAIR), PAIR), lanes : lanes + LANES] = (
                    jnp.concatenate(parts, axis=0).astype(out_rows.dtype)
                )
            return states

        lax.fori_loop(0, length // PAIR, step, tuple(carried[m, n] for n in range(modes)))
        write(m).start()

    for m in range(groups):
        feature(m)
    pl.semaphore_wait(barrier, n_seq + n_chan - 2)
    for m in range(groups):
        gather_states(m)
        send_states(m)
        if m >= 1:
            scan_group(m - 1)
        if m >= 2:
            scan_all(m - 2)
    for m in range(groups):
        convolve(m)
        if m == 0:
            scan_group(groups - 1)
            scan_all(groups - 2)
        if m == 1:
            scan_all(groups - 1)
    for m in range(groups):
        write(m).wait()
        wait_bytes(got_state, n_seq - 1, m, send_state)
        wait_bytes(got_total, n_chan - 1, m, send_total)
        wait_bytes(carried, n_seq - 1, m, send_back)


def shards(n_chan, n_seq, projected, short_filter, residues, decays, skip):
    _, length, width = projected.shape
    modes = residues.shape[0]
    groups = width // WIDE
    axes = ("chan", "seq")
    packed = jnp.concatenate([residues * jnp.sqrt(decays), decays, skip[None]], axis=0)
    params = lax.all_gather(packed, axes, axis=1, tiled=True)
    params = params.reshape(2 * modes + 1, groups, ROWS, LANES)
    count = n_chan * n_seq
    halo = lax.ppermute(projected[:, -2:, :], axes, [(i, i + 1) for i in range(count - 1)])
    halo = halo.astype(F32).reshape(6, groups, ROWS, LANES)
    filt = short_filter.reshape(9, groups, ROWS, LANES)
    vmem = pl.BlockSpec(memory_space=pltpu.VMEM)
    hbm = pl.BlockSpec(memory_space=pl.ANY)
    dma = pltpu.SemaphoreType.DMA
    blocks = length // BLOCK
    return pl.pallas_call(
        functools.partial(kernel, n_chan, n_seq),
        out_shape=jax.ShapeDtypeStruct((length, width), projected.dtype),
        in_specs=[hbm] + [vmem] * 5,
        out_specs=hbm,
        scratch_shapes=[
            pltpu.VMEM((3, length, width), projected.dtype),
            pltpu.VMEM((3, PAIR * ROWS, LANES), F32),
            pltpu.VMEM((groups, length * ROWS, LANES), F32),
            pltpu.VMEM((groups, length * ROWS, LANES), F32),
            pltpu.VMEM((groups, blocks, modes, ROWS, LANES), F32),
            pltpu.VMEM((modes, groups, ROWS, LANES), F32),
            pltpu.VMEM((modes, groups, ROWS, LANES), F32),
            pltpu.VMEM((BLOCK, ROWS, LANES), F32),
            pltpu.VMEM((groups, modes, ROWS, LANES), F32),
            pltpu.VMEM((groups, n_seq, ROWS, LANES), F32),
            pltpu.VMEM((groups, n_seq, ROWS, LANES), F32),
            pltpu.VMEM((groups, ROWS, LANES), F32),
            pltpu.VMEM((groups, n_chan, ROWS, LANES), F32),
            pltpu.VMEM((groups, n_seq, ROWS, LANES), F32),
            pltpu.VMEM((groups, modes, ROWS, LANES), F32),
            pltpu.VMEM((PAIR * ROWS, LANES), F32),
            pltpu.VMEM((length, width), projected.dtype),
            dma((groups, 3)),
            dma((groups,)),
            dma((groups,)),
            dma((groups,)),
            dma((groups,)),
            dma((groups,)),
            dma((groups,)),
            dma((groups,)),
        ],
        compiler_params=pltpu.CompilerParams(
            collective_id=0, has_side_effects=True, vmem_limit_bytes=48 * 1024 * 1024
        ),
        name="hyena",
    )(projected, filt, params[:modes], params[modes : 2 * modes], params[2 * modes], halo)


def solution(mesh):
    return jax.shard_map(
        functools.partial(shards, mesh.shape["chan"], mesh.shape["seq"]),
        mesh=mesh,
        in_specs=(
            P(None, ("chan", "seq"), None),
            P(),
            P(None, ("chan", "seq")),
            P(None, ("chan", "seq")),
            P(("chan", "seq")),
        ),
        out_specs=P(("chan", "seq"), None),
        check_vma=False,
    )
```

time: 490 us -> 230 us (0.47); the launches traced: 483 us -> 230 us
  other arithmetic: 270 us -> 1.45 us
  blocking collectives: 39.9 us -> 183 us
  matrix products: 131 us -> 0 us
  Pallas kernels: 0 us -> 31.9 us
  local copies, waits for them, and re-layouts: 26.8 us -> 8.5 us
  starting transfers between devices: 15.4 us -> 4.94 us
    sub x16 -> x0, other arithmetic: 190 us -> none  [add_mode(): return (spec_real + scaled * denom_real, spec_imag - scaled * denom_imag)]
    all_gather x0 -> x1, blocking collectives: none -> 183 us  [shards(): params = lax.all_gather(packed, axes, axis=1, tiled=True)]
    dot_general x12 -> x0, matrix products: 131 us -> none  [the longest x1 27.5 us: convolve(): jnp.einsum('ckm,mj->ckj', turned_imag, cos_two, precision=precise)]
    all_to_all x1 -> x0, blocking collectives: 39.9 us -> none  [shards(): lax.all_to_all(conv, ('chan', 'seq'), split_axis=1, concat_axis=0, tiled=...]
    pallas_call x0 -> x1, Pallas kernels: none -> 31.9 us  [shards(): pl.pallas_call(functools.partial(kernel, n_chan, n_seq), out_shape=jax.Sh...]
    sin x17 -> x0, other arithmetic: 28.6 us -> none  [the longest x16 27.6 us: convolve(): sine_full = jnp.sin(frequency * (2.0 * math.pi / n_total))]
    convert_element_type x19 -> x0, other arithmetic: 20.3 us -> none  [the longest x1 13 us: shards(): jnp.concatenate([before_rows, projected], axis=1).astype(jnp.float32)]
    add x2 -> x0, other arithmetic: 18.2 us -> none  [the longest x1 18.2 us: shards(): short_filter[:, 0, None, :] * extended[:, 2:]]
  transfers between devices with their start and end apart: 2 -> 1, of which waited for: 0 -> 0; matrix products, arithmetic and copies ran while one was open for 51% -> 3% of each run, Pallas kernels for 0% -> 0%
where the time goes in v1:
time: 230 us
  blocking collectives  183 us (80%)
  Pallas kernels  31.9 us (14%)
  local copies, waits for them, and re-layouts  8.5 us (4%)
  starting transfers between devices  4.94 us (2%)
    all_gather x1, blocking collectives, shards(): params = lax.all_gather(packed, axes, axis=1, tiled=True)  183 us
    pallas_call x1, Pallas kernels, shards(): pl.pallas_call(functools.partial(kernel, n_chan, n_seq), out_shape=jax.Sh...  31.9 us
    ppermute x1, starting transfers between devices, shards(): lax.ppermute(projected[:, -2:, :], axes, [(i, i + 1) for i in range(count...  4.94 us
  transfers between devices with their start and end apart: 1, of which 0 were waited for; matrix products, arithmetic and copies ran while one was open for 3% of the time, Pallas kernels for 0%

profile of v1, /device:TPU:1, one launch (start us, length us, event | category | flops | bytes accessed | tf_op | source)
XLA Modules:
  0.0 229.5 jit_solution(5788008602495854940)
XLA Ops:
  0.0 1.0 slice.24
  1.0 4.9 %collective-permute-start = (bf16[3,2,4096]{2,1,0:T(2,128)(2,1)S(1)}, bf16[3,2,4096]{2,1,0:T(2,128)(2,1)S(1)}, u32[]{:S(2)}, u32[]{:S(2)}) collective-permute-start(bf16[3,2,4096]{2,1,0:T(2,128)(2,1)S(1)} %slice.24), channel_id=1, source_target_pairs={{0,1},{1,2},{2,3},{3,4},{4,5},{5,6},{6,7},{7,8},{8,9},{9,10},{10,1... | collective-permute-start | bytes 147464 | tf_op jit(solution)/shard_map/ppermute | solution.py:292
  5.9 0.7 sqrt_multiply_fusion
  6.7 0.7 pad_maximum_fusion
  7.4 0.1 copy.18
  7.5 182.7 %all_gather.3 = f32[33,4096]{0,1:T(8,128)S(1)} all-gather(f32[33,32]{0,1:T(8,128)S(1)} %copy.18), channel_id=1, replica_groups=mesh['chan'=8,'seq'=16] {'chan','seq'}, dimensions={1}, use_global_device_ids=true | all-gather | bytes 544896 | tf_op jit(solution)/shard_map/all_gather | solution.py:289
  190.2 2.0 fusion
  192.1 0.0 copy-start
  192.1 1.2 slice_reduce_fusion
  193.3 0.0 copy-done
  193.3 0.1 reshape.13.filt
  193.4 2.2 copy.22.decay
  195.6 0.6 copy.21.weight
  196.3 0.0 collective-permute-done
  196.3 31.9 %hyena.1 = bf16[256,4096]{1,0:T(8,128)(2,1)S(1)} custom-call(bf16[3,256,4096]{2,1,0:T(8,128)(2,1)} %x_hbm.1, f32[9,4,8,128]{3,2,1,0:T(8,128)S(1)} %reshape.13.filt, f32[16,4,8,128]{3,2,1,0:T(8,128)S(1)} %copy.21.weight, f32[16,4,8,128]{3,2,1,0:T(8,128)S(1)} %copy.22.decay, f32[4,8,128]{2,1,0:T(8,128)S(1)} %bitcast.4, f32[6,4,8,128]{3,2,1,0:T(8,128)S(1)} %reshape.17.halo), custom_call_target="tpu_custom_call" | custom-call | tf_op jit(solution)/shard_map/hyena/pallas_call | solution.py:299
  228.2 1.3 copy.24
  (1 shorter events, 0.0 us)
Async XLA Ops:
  1.0 195.3 %collective-permute-start = (bf16[3,2,4096]{2,1,0:T(2,128)(2,1)S(1)}, bf16[3,2,4096]{2,1,0:T(2,128)(2,1)S(1)}, u32[]{:S(2)}, u32[]{:S(2)}) collective-permute-start(bf16[3,2,4096]{2,1,0:T(2,128)(2,1)S(1)} %slice.24), channel_id=1, source_target_pairs={{0,1},{1,2},{2,3},{3,4},{4,5},{5,6},{6,7},{7,8},{8,9},{9,10},{10,1... | collective-permute-start | bytes 147464 | tf_op jit(solution)/shard_map/ppermute | solution.py:292
  192.1 1.2 copy-start

commit v2 on v1

--- a/solution.py
+++ b/solution.py
@@ -25,16 +25,22 @@
     n_seq,
     x_hbm,
     filt,
-    weight,
-    decay,
-    skip,
-    halo,
+    residues,
+    rates,
+    direct,
     out_hbm,
     xb,
     tiles,
     gated,
     queries,
     ends,
+    params,
+    weight,
+    decay,
+    skip,
+    last,
+    halo,
+    head,
     power,
     power_block,
     taps,
@@ -49,6 +55,12 @@
     out_rows,
     in_sem,
     out_sem,
+    send_near,
+    recv_near,
+    send_far,
+    recv_far,
+    send_halo,
+    recv_halo,
     send_state,
     recv_state,
     send_total,
@@ -59,8 +71,13 @@
     groups = gated.shape[0]
     length = x_hbm.shape[1]
     modes = weight.shape[0]
+    share = n_chan // groups
     my_chan = lax.axis_index("chan")
     my_seq = lax.axis_index("seq")
+    count = n_chan * n_seq
+    mine = my_chan * n_seq + my_seq
+    after = lax.rem(mine + 1, count)
+    ahead = lax.rem(mine + count - 1, count)
 
     def fetch(j, m):
         columns = pl.ds(m * WIDE, WIDE)
@@ -79,9 +96,113 @@
     for off in range(1, n_chan):
         peer = lax.rem(my_chan + off, n_chan)
         pl.semaphore_signal(barrier, inc=1, device_id=(peer, my_seq), device_id_type=MESH)
-
-    power[...] = jnp.exp(-decay[...])
-    power_block[...] = jnp.exp(-float(BLOCK) * decay[...])
+    pl.semaphore_signal(
+        barrier, inc=1, device_id=(ahead // n_seq, ahead % n_seq), device_id_type=MESH
+    )
+
+    part = residues.shape[1]
+    quads = LANES // part
+    half = modes // quads
+    for r in range(half):
+        for b in range(quads):
+            n = r * quads + b
+            lanes = slice(b * part, (b + 1) * part)
+            params[mine, r : r + 1, lanes] = residues[n : n + 1, :] * jnp.sqrt(rates[n : n + 1, :])
+            params[mine, half + r : half + r + 1, lanes] = rates[n : n + 1, :]
+    params[mine, 2 * half : 2 * half + 1, 0:part] = direct[...]
+    params[mine, 2 * half : 2 * half + 1, part:] = jnp.zeros((1, LANES - part), F32)
+
+    def near_copy(off):
+        peer = lax.rem(my_chan + off, n_chan)
+        return pltpu.make_async_remote_copy(
+            src_ref=params.at[mine],
+            dst_ref=params.at[mine],
+            send_sem=send_near,
+            recv_sem=recv_near,
+            device_id=(peer, my_seq),
+            device_id_type=MESH,
+        )
+
+    def far_copy(c, off):
+        peer = lax.rem(my_seq + off, n_seq)
+        place = params.at[c * n_seq + my_seq]
+        return pltpu.make_async_remote_copy(
+            src_ref=place,
+            dst_ref=place,
+            send_sem=send_far.at[c // share],
+            recv_sem=recv_far.at[c // share],
+            device_id=(my_chan, peer),
+            device_id_type=MESH,
+        )
+
+    def halo_copy(m):
+        return pltpu.make_async_remote_copy(
+            src_ref=last.at[m],
+            dst_ref=halo.at[m],
+            send_sem=send_halo.at[m],
+            recv_sem=recv_halo.at[m],
+            device_id=(after // n_seq, after % n_seq),
+            device_id_type=MESH,
+        )
+
+    def spread_params(m):
+        some = params.at[pl.ds(0, (n_seq - 1) * share)]
+        pltpu.make_async_copy(some, some, recv_far.at[m]).wait()
+        group = lax.broadcasted_iota(jnp.int32, (ROWS, LANES), 1) // part
+        depth = params.shape[1]
+
+        def pick(row):
+            found = []
+            for i in range(quads):
+                found.append(
+                    jnp.concatenate(
+                        [
+                            params[(m * ROWS + j) * quads + i, row : row + 1, :]
+                            for j in range(ROWS)
+                        ],
+                        axis=0,
+                    )
+                )
+            return found
+
+        def place(found, b):
+            value = None
+            for i in range(quads):
+                shift = (i - b) % quads * part
+                turned = pltpu.roll(found[i], shift, 1) if shift else found[i]
+                value = turned if i == 0 else jnp.where(group == i, turned, value)
+            return value
+
+        for r in range(half):
+            heavy = pick(r)
+            rate = pick(half + r)
+            for b in range(quads):
+                n = r * quads + b
+                weight[n, m] = place(heavy, b)
+                value = place(rate, b)
+                decay[n, m] = value
+                power[n, m] = jnp.exp(-value)
+                power_block[n, m] = jnp.exp(-float(BLOCK) * value)
+        skip[m] = place(pick(2 * half), 0)
+
+    def patch(m):
+        halo_copy(m).wait_recv()
+        for t in range(2):
+            featured = []
+            for j in range(3):
+                rows = [
+                    jnp.where(mine > 0, halo[m, 2 * j], 0.0),
+                    jnp.where(mine > 0, halo[m, 2 * j + 1], 0.0),
+                    head[m, 2 * j],
+                    head[m, 2 * j + 1],
+                ]
+                featured.append(
+                    filt[3 * j, m] * rows[t + 2]
+                    + filt[3 * j + 1, m] * rows[t + 1]
+                    + filt[3 * j + 2, m] * rows[t]
+                )
+            queries[m, t * ROWS : (t + 1) * ROWS, :] = featured[0]
+            gated[m, t * ROWS : (t + 1) * ROWS, :] = featured[1] * featured[2]
 
     def feature(m):
         for j in range(3):
@@ -111,7 +232,17 @@
                 gated[m, place, :] = featured[1] * featured[2]
             return tuple(olds)
 
-        lax.fori_loop(0, length // PAIR, step, tuple(halo[i, m] for i in range(6)))
+        zero = jnp.zeros((ROWS, LANES), F32)
+        olds = lax.fori_loop(0, length // PAIR, step, (zero,) * 6)
+        for i in range(6):
+            last[m, i] = olds[i]
+        halo_copy(m).start()
+        for j in range(3):
+            rows = xb[j, 0:PAIR, m * WIDE : (m + 1) * WIDE].astype(F32)[:ROWS]
+            for i in range(ROWS):
+                tiles[j, i * ROWS : (i + 1) * ROWS, :] = rows[:, i * LANES : (i + 1) * LANES]
+            for t in range(2):
+                head[m, 2 * j + t] = tiles[j, token(t), :]
 
     def gather_states(m):
         def step(b, states):
@@ -256,10 +387,20 @@
         lax.fori_loop(0, length // PAIR, step, tuple(carried[m, n] for n in range(modes)))
         write(m).start()
 
+    pl.semaphore_wait(barrier, n_seq + n_chan - 1)
+    for off in range(1, n_chan):
+        near_copy(off).start()
     for m in range(groups):
         feature(m)
-    pl.semaphore_wait(barrier, n_seq + n_chan - 2)
+        if m == 0:
+            some = params.at[pl.ds(0, n_chan - 1)]
+            pltpu.make_async_copy(some, some, recv_near).wait()
+            for c in range(n_chan):
+                for off in range(1, n_seq):
+                    far_copy(c, off).start()
     for m in range(groups):
+        patch(m)
+        spread_params(m)
         gather_states(m)
         send_states(m)
         if m >= 1:
@@ -273,8 +414,13 @@
             scan_all(groups - 2)
         if m == 1:
             scan_all(groups - 1)
+    some = params.at[pl.ds(0, n_chan - 1)]
+    pltpu.make_async_copy(some, some, send_near).wait()
+    some = params.at[pl.ds(0, (n_seq - 1) * share)]
     for m in range(groups):
         write(m).wait()
+        halo_copy(m).wait_send()
+        pltpu.make_async_copy(some, some, send_far.at[m]).wait()
         wait_bytes(got_state, n_seq - 1, m, send_state)
         wait_bytes(got_total, n_chan - 1, m, send_total)
         wait_bytes(carried, n_seq - 1, m, send_back)
@@ -284,13 +430,6 @@
     _, length, width = projected.shape
     modes = residues.shape[0]
     groups = width // WIDE
-    axes = ("chan", "seq")
-    packed = jnp.concatenate([residues * jnp.sqrt(decays), decays, skip[None]], axis=0)
-    params = lax.all_gather(packed, axes, axis=1, tiled=True)
-    params = params.reshape(2 * modes + 1, groups, ROWS, LANES)
-    count = n_chan * n_seq
-    halo = lax.ppermute(projected[:, -2:, :], axes, [(i, i + 1) for i in range(count - 1)])
-    halo = halo.astype(F32).reshape(6, groups, ROWS, LANES)
     filt = short_filter.reshape(9, groups, ROWS, LANES)
     vmem = pl.BlockSpec(memory_space=pltpu.VMEM)
     hbm = pl.BlockSpec(memory_space=pl.ANY)
@@ -299,7 +438,7 @@
     return pl.pallas_call(
         functools.partial(kernel, n_chan, n_seq),
         out_shape=jax.ShapeDtypeStruct((length, width), projected.dtype),
-        in_specs=[hbm] + [vmem] * 5,
+        in_specs=[hbm] + [vmem] * 4,
         out_specs=hbm,
         scratch_shapes=[
             pltpu.VMEM((3, length, width), projected.dtype),
@@ -307,6 +446,13 @@
             pltpu.VMEM((groups, length * ROWS, LANES), F32),
             pltpu.VMEM((groups, length * ROWS, LANES), F32),
             pltpu.VMEM((groups, blocks, modes, ROWS, LANES), F32),
+            pltpu.VMEM((n_chan * n_seq, 2 * ROWS, LANES), F32),
+            pltpu.VMEM((modes, groups, ROWS, LANES), F32),
+            pltpu.VMEM((modes, groups, ROWS, LANES), F32),
+            pltpu.VMEM((groups, ROWS, LANES), F32),
+            pltpu.VMEM((groups, 6, ROWS, LANES), F32),
+            pltpu.VMEM((groups, 6, ROWS, LANES), F32),
+            pltpu.VMEM((groups, 6, ROWS, LANES), F32),
             pltpu.VMEM((modes, groups, ROWS, LANES), F32),
             pltpu.VMEM((modes, groups, ROWS, LANES), F32),
             pltpu.VMEM((BLOCK, ROWS, LANES), F32),
@@ -321,6 +467,12 @@
             pltpu.VMEM((length, width), projected.dtype),
             dma((groups, 3)),
             dma((groups,)),
+            dma,
+            dma,
+            dma((groups,)),
+            dma((groups,)),
+            dma((groups,)),
+            dma((groups,)),
             dma((groups,)),
             dma((groups,)),
             dma((groups,)),
@@ -332,7 +484,7 @@
             collective_id=0, has_side_effects=True, vmem_limit_bytes=48 * 1024 * 1024
         ),
         name="hyena",
-    )(projected, filt, params[:modes], params[modes : 2 * modes], params[2 * modes], halo)
+    )(projected, filt, residues, decays, skip[None])
 
 
 def solution(mesh):

time: 230 us -> 54.9 us (0.24)
  blocking collectives: 183 us -> 0 us
  Pallas kernels: 31.9 us -> 50.3 us
  starting transfers between devices: 4.94 us -> 0 us
  local copies, waits for them, and re-layouts: 8.5 us -> 4.4 us
    all_gather x1 -> x0, blocking collectives: 183 us -> none  [shards(): params = lax.all_gather(packed, axes, axis=1, tiled=True)]
    pallas_call x1, Pallas kernels: 31.9 us -> 50.3 us  [shards(): pl.pallas_call(functools.partial(kernel, n_chan, n_seq), out_shape=jax.Sh...]
    slice x5 -> x0, local copies, waits for them, and re-layouts: 6.95 us -> none  [the longest x2 4.18 us: shards(): params[modes:2 * modes]]
    ppermute x1 -> x0, starting transfers between devices: 4.94 us -> none  [shards(): lax.ppermute(projected[:, -2:, :], axes, [(i, i + 1) for i in range(count...]
  transfers between devices with their start and end apart: 1 -> 0, of which waited for: 0 -> 0; matrix products, arithmetic and copies ran while one was open for 3% -> 0% of each run, Pallas kernels for 0% -> 0%
where the time goes in v2:
time: 54.9 us; the launch traced here: 54.7 us
  Pallas kernels  50.3 us (92%)
  local copies, waits for them, and re-layouts  4.4 us (8%)
    pallas_call x1, Pallas kernels, shards(): pl.pallas_call(functools.partial(kernel, n_chan, n_seq), out_shape=jax.Sh...  50.3 us
    unnamed x7, local copies, waits for them, and re-layouts  3.36 us

profile of v2, /device:TPU:1, one launch (start us, length us, event | category | flops | bytes accessed | tf_op | source)
XLA Modules:
  0.0 54.7 jit_solution(7089019197211404202)
XLA Ops:
  0.0 1.0 %reshape.3.filt = f32[9,4,8,128]{3,2,1,0:T(8,128)S(1)} reshape(f32[3,3,4096]{2,1,0:T(4,128)} %param.6) | data formatting | bytes 294912 | tf_op jit(solution)/shard_map/reshape | solution.py:433
  1.0 0.0 copy-start
  1.1 0.7 %copy-done = f32[16,32]{1,0:T(8,128)S(1)} copy-done((f32[16,32]{1,0:T(8,128)S(1)}, f32[16,32]{1,0:T(8,128)}, u32[]{:S(2)}) %copy-start) | copy-done | bytes 2072
  1.7 0.0 copy-start.1
  1.7 0.7 %copy-done.1 = f32[16,32]{1,0:T(8,128)S(1)} copy-done((f32[16,32]{1,0:T(8,128)S(1)}, f32[16,32]{1,0:T(8,128)}, u32[]{:S(2)}) %copy-start.1) | copy-done | bytes 2072
  2.4 0.0 copy-start.2
  2.4 0.7 %copy-done.2 = f32[32]{0:T(128)S(1)} copy-done((f32[32]{0:T(128)S(1)}, f32[32]{0:T(128)}, u32[]{:S(2)}) %copy-start.2) | copy-done | bytes 152
  3.1 50.3 %hyena.1 = bf16[256,4096]{1,0:T(8,128)(2,1)S(1)} custom-call(bf16[3,256,4096]{2,1,0:T(8,128)(2,1)} %x_hbm.1, f32[9,4,8,128]{3,2,1,0:T(8,128)S(1)} %reshape.3.filt, f32[16,32]{1,0:T(8,128)S(1)} %copy-done, f32[16,32]{1,0:T(8,128)S(1)} %copy-done.1, f32[1,32]{1,0:T(1,128)S(1)} %bitcast.1), custom_call_target="tpu_custom_call" | custom-call | tf_op jit(solution)/shard_map/hyena/pallas_call | solution.py:438
  53.4 1.3 %copy.7 = bf16[256,4096]{1,0:T(8,128)(2,1)} copy(bf16[256,4096]{1,0:T(8,128)(2,1)S(1)} %hyena.1) | data formatting | bytes 4194304
Async XLA Ops:
  1.0 0.7 %copy-start = (f32[16,32]{1,0:T(8,128)S(1)}, f32[16,32]{1,0:T(8,128)}, u32[]{:S(2)}) copy-start(f32[16,32]{1,0:T(8,128)} %residues.1) | copy-start | bytes 6148
  1.7 0.7 %copy-start.1 = (f32[16,32]{1,0:T(8,128)S(1)}, f32[16,32]{1,0:T(8,128)}, u32[]{:S(2)}) copy-start(f32[16,32]{1,0:T(8,128)} %rates.1) | copy-start | bytes 6148
  2.4 0.7 %copy-start.2 = (f32[32]{0:T(128)S(1)}, f32[32]{0:T(128)}, u32[]{:S(2)}) copy-start(f32[32]{0:T(128)} %param.9) | copy-start | bytes 388

commit v3 on v2

--- a/solution.py
+++ b/solution.py
@@ -24,12 +24,17 @@
     n_chan,
     n_seq,
     x_hbm,
+    filt_hbm,
+    residues_hbm,
+    rates_hbm,
+    direct_hbm,
+    out_hbm,
+    xb,
+    filt_rows,
     filt,
     residues,
     rates,
     direct,
-    out_hbm,
-    xb,
     tiles,
     gated,
     queries,
@@ -54,6 +59,7 @@
     out_tiles,
     out_rows,
     in_sem,
+    small_sem,
     out_sem,
     send_near,
     recv_near,
@@ -71,7 +77,6 @@
     groups = gated.shape[0]
     length = x_hbm.shape[1]
     modes = weight.shape[0]
-    share = n_chan // groups
     my_chan = lax.axis_index("chan")
     my_seq = lax.axis_index("seq")
     count = n_chan * n_seq
@@ -85,20 +90,52 @@
             x_hbm.at[j, :, columns], xb.at[j, :, columns], in_sem.at[m, j]
         )
 
+    small = [
+        pltpu.make_async_copy(source, place, small_sem.at[i])
+        for i, (source, place) in enumerate(
+            [
+                (residues_hbm, residues),
+                (rates_hbm, rates),
+                (direct_hbm, direct),
+                (filt_hbm, filt_rows),
+            ]
+        )
+    ]
+    for copy in small:
+        copy.start()
     for m in range(groups):
         for j in range(3):
             fetch(j, m).start()
 
+    chips = count // 2
+    my_chip = mine // 2
+    my_core = mine % 2
+    other = 1 - my_core
+
+    def device(chip, core):
+        per = n_seq // 2
+        return chip // per, chip % per * 2 + core
+
+    def signal(target):
+        pl.semaphore_signal(barrier, inc=1, device_id=target, device_id_type=MESH)
+
     barrier = pltpu.get_barrier_semaphore()
-    for off in range(1, n_seq):
-        peer = lax.rem(my_seq + off, n_seq)
-        pl.semaphore_signal(barrier, inc=1, device_id=(my_chan, peer), device_id_type=MESH)
-    for off in range(1, n_chan):
-        peer = lax.rem(my_chan + off, n_chan)
-        pl.semaphore_signal(barrier, inc=1, device_id=(peer, my_seq), device_id_type=MESH)
-    pl.semaphore_signal(
-        barrier, inc=1, device_id=(ahead // n_seq, ahead % n_seq), device_id_type=MESH
-    )
+    for off in range(1, chips):
+        signal(device(lax.rem(my_chip + off, chips), my_core))
+    first_chip = my_chip - my_chip % (n_seq // 2)
+    for off in range(n_seq // 2):
+        signal(device(first_chip + off, other))
+    signal((ahead // n_seq, ahead % n_seq))
+    signals = chips - 1 + n_seq // 2 + 1
+
+    for copy in small:
+        copy.wait()
+    for j in range(3):
+        for tap in range(3):
+            for m in range(groups):
+                for i in range(ROWS):
+                    lanes = slice(m * WIDE + i * LANES, m * WIDE + (i + 1) * LANES)
+                    filt[3 * j + tap, m, i : i + 1, :] = filt_rows[j, tap : tap + 1, lanes]
 
     part = residues.shape[1]
     quads = LANES // part
@@ -107,31 +144,36 @@
         for b in range(quads):
             n = r * quads + b
             lanes = slice(b * part, (b + 1) * part)
-            params[mine, r : r + 1, lanes] = residues[n : n + 1, :] * jnp.sqrt(rates[n : n + 1, :])
-            params[mine, half + r : half + r + 1, lanes] = rates[n : n + 1, :]
-    params[mine, 2 * half : 2 * half + 1, 0:part] = direct[...]
-    params[mine, 2 * half : 2 * half + 1, part:] = jnp.zeros((1, LANES - part), F32)
+            params[my_chip, my_core, r : r + 1, lanes] = residues[n : n + 1, :] * jnp.sqrt(rates[n : n + 1, :])
+            params[my_chip, my_core, half + r : half + r + 1, lanes] = rates[n : n + 1, :]
+    params[my_chip, my_core, 2 * half : 2 * half + 1, 0:part] = direct[...]
+    params[my_chip, my_core, 2 * half : 2 * half + 1, part:] = jnp.zeros((1, LANES - part), F32)
+
+    used = pl.ds(0, 2 * half + 1)
 
     def near_copy(off):
-        peer = lax.rem(my_chan + off, n_chan)
-        return pltpu.make_async_remote_copy(
-            src_ref=params.at[mine],
-            dst_ref=params.at[mine],
-            send_sem=send_near,
-            recv_sem=recv_near,
-            device_id=(peer, my_seq),
-            device_id_type=MESH,
-        )
-
-    def far_copy(c, off):
-        peer = lax.rem(my_seq + off, n_seq)
-        place = params.at[c * n_seq + my_seq]
+        place = params.at[my_chip, my_core, used]
         return pltpu.make_async_remote_copy(
             src_ref=place,
             dst_ref=place,
-            send_sem=send_far.at[c // share],
-            recv_sem=recv_far.at[c // share],
-            device_id=(my_chan, peer),
+            send_sem=send_near,
+            recv_sem=recv_near,
+            device_id=device(lax.rem(my_chip + off, chips), my_core),
+            device_id_type=MESH,
+        )
+
+    def wait_near(sem):
+        some = params.at[pl.ds(0, chips - 1), 0, used]
+        pltpu.make_async_copy(some, some, sem).wait()
+
+    def far_copy(m):
+        place = params.at[pl.ds(m * (chips // groups), chips // groups), my_core, used]
+        return pltpu.make_async_remote_copy(
+            src_ref=place,
+            dst_ref=place,
+            send_sem=send_far.at[m],
+            recv_sem=recv_far.at[m],
+            device_id=device(my_chip, other),
             device_id_type=MESH,
         )
 
@@ -146,10 +188,8 @@
         )
 
     def spread_params(m):
-        some = params.at[pl.ds(0, (n_seq - 1) * share)]
-        pltpu.make_async_copy(some, some, recv_far.at[m]).wait()
+        far_copy(m).wait_recv()
         group = lax.broadcasted_iota(jnp.int32, (ROWS, LANES), 1) // part
-        depth = params.shape[1]
 
         def pick(row):
             found = []
@@ -157,7 +197,7 @@
                 found.append(
                     jnp.concatenate(
                         [
-                            params[(m * ROWS + j) * quads + i, row : row + 1, :]
+                            params[((m * ROWS + j) * quads + i) // 2, i % 2, row : row + 1, :]
                             for j in range(ROWS)
                         ],
                         axis=0,
@@ -387,40 +427,33 @@
         lax.fori_loop(0, length // PAIR, step, tuple(carried[m, n] for n in range(modes)))
         write(m).start()
 
-    pl.semaphore_wait(barrier, n_seq + n_chan - 1)
-    for off in range(1, n_chan):
+    pl.semaphore_wait(barrier, signals)
+    for off in range(1, chips):
         near_copy(off).start()
     for m in range(groups):
         feature(m)
-        if m == 0:
-            some = params.at[pl.ds(0, n_chan - 1)]
-            pltpu.make_async_copy(some, some, recv_near).wait()
-            for c in range(n_chan):
-                for off in range(1, n_seq):
-                    far_copy(c, off).start()
+    wait_near(recv_near)
+    for m in range(groups):
+        far_copy(m).start()
     for m in range(groups):
         patch(m)
         spread_params(m)
         gather_states(m)
         send_states(m)
-        if m >= 1:
-            scan_group(m - 1)
+    scan_group(0)
+    for m in range(1, groups):
+        scan_group(m)
         if m >= 2:
             scan_all(m - 2)
+    scan_all(groups - 2)
+    scan_all(groups - 1)
     for m in range(groups):
         convolve(m)
-        if m == 0:
-            scan_group(groups - 1)
-            scan_all(groups - 2)
-        if m == 1:
-            scan_all(groups - 1)
-    some = params.at[pl.ds(0, n_chan - 1)]
-    pltpu.make_async_copy(some, some, send_near).wait()
-    some = params.at[pl.ds(0, (n_seq - 1) * share)]
+    wait_near(send_near)
     for m in range(groups):
         write(m).wait()
         halo_copy(m).wait_send()
-        pltpu.make_async_copy(some, some, send_far.at[m]).wait()
+        far_copy(m).wait_send()
         wait_bytes(got_state, n_seq - 1, m, send_state)
         wait_bytes(got_total, n_chan - 1, m, send_total)
         wait_bytes(carried, n_seq - 1, m, send_back)
@@ -430,23 +463,26 @@
     _, length, width = projected.shape
     modes = residues.shape[0]
     groups = width // WIDE
-    filt = short_filter.reshape(9, groups, ROWS, LANES)
-    vmem = pl.BlockSpec(memory_space=pltpu.VMEM)
-    hbm = pl.BlockSpec(memory_space=pl.ANY)
+    hbm = pl.BlockSpec(memory_space=pltpu.HBM)
     dma = pltpu.SemaphoreType.DMA
     blocks = length // BLOCK
     return pl.pallas_call(
         functools.partial(kernel, n_chan, n_seq),
         out_shape=jax.ShapeDtypeStruct((length, width), projected.dtype),
-        in_specs=[hbm] + [vmem] * 4,
-        out_specs=hbm,
+        in_specs=[hbm] * 5,
+        out_specs=pl.BlockSpec(memory_space=pl.ANY),
         scratch_shapes=[
             pltpu.VMEM((3, length, width), projected.dtype),
+            pltpu.VMEM(short_filter.shape, F32),
+            pltpu.VMEM((9, groups, ROWS, LANES), F32),
+            pltpu.VMEM(residues.shape, F32),
+            pltpu.VMEM(decays.shape, F32),
+            pltpu.VMEM((1, skip.shape[0]), F32),
             pltpu.VMEM((3, PAIR * ROWS, LANES), F32),
             pltpu.VMEM((groups, length * ROWS, LANES), F32),
             pltpu.VMEM((groups, length * ROWS, LANES), F32),
             pltpu.VMEM((groups, blocks, modes, ROWS, LANES), F32),
-            pltpu.VMEM((n_chan * n_seq, 2 * ROWS, LANES), F32),
+            pltpu.VMEM((n_chan * n_seq // 2, 2, 2 * ROWS, LANES), F32),
             pltpu.VMEM((modes, groups, ROWS, LANES), F32),
             pltpu.VMEM((modes, groups, ROWS, LANES), F32),
             pltpu.VMEM((groups, ROWS, LANES), F32),
@@ -466,6 +502,7 @@
             pltpu.VMEM((PAIR * ROWS, LANES), F32),
             pltpu.VMEM((length, width), projected.dtype),
             dma((groups, 3)),
+            dma((4,)),
             dma((groups,)),
             dma,
             dma,
@@ -484,7 +521,7 @@
             collective_id=0, has_side_effects=True, vmem_limit_bytes=48 * 1024 * 1024
         ),
         name="hyena",
-    )(projected, filt, residues, decays, skip[None])
+    )(projected, *[pltpu.with_memory_space_constraint(v, pltpu.HBM) for v in (short_filter, residues, decays, skip[None])])
 
 
 def solution(mesh):

time: 54.9 us -> 44.9 us (0.82)
  Pallas kernels: 50.3 us -> 43.5 us
  local copies, waits for them, and re-layouts: 4.4 us -> 1.32 us
    pallas_call x1, Pallas kernels: 50.3 us -> 43.5 us  [shards(): pl.pallas_call(functools.partial(kernel, n_chan, n_seq), out_shape=jax.Sh...]
    unnamed x7 -> x1, local copies, waits for them, and re-layouts: 3.36 us -> 1.32 us
    reshape x1 -> x0, local copies, waits for them, and re-layouts: 1.04 us -> none  [shards(): filt = short_filter.reshape(9, groups, ROWS, LANES)]
where the time goes in v3:
time: 44.9 us; the launch traced here: 44.8 us
  Pallas kernels  43.5 us (97%)
  local copies, waits for them, and re-layouts  1.32 us (3%)
    pallas_call x1, Pallas kernels, shards(): pl.pallas_call(functools.partial(kernel, n_chan, n_seq), out_shape=jax.Sh...  43.5 us
    unnamed x1, local copies, waits for them, and re-layouts  1.32 us

profile of v3, /device:TPU:1, one launch (start us, length us, event | category | flops | bytes accessed | tf_op | source)
XLA Modules:
  0.0 44.8 jit_solution(6905366810160671298)
XLA Ops:
  0.0 43.5 %hyena.1 = bf16[256,4096]{1,0:T(8,128)(2,1)S(1)} custom-call(bf16[3,256,4096]{2,1,0:T(8,128)(2,1)} %x_hbm.1, f32[3,3,4096]{2,1,0:T(4,128)} %filt_hbm.1, f32[16,32]{1,0:T(8,128)} %residues_hbm.1, f32[16,32]{1,0:T(8,128)} %rates_hbm.1, f32[1,32]{1,0:T(1,128)} %bitcast.1), custom_call_target="tpu_custom_call" | custom-call | tf_op jit(solution)/shard_map/hyena/pallas_call | solution.py:469
  43.5 1.3 %copy.7 = bf16[256,4096]{1,0:T(8,128)(2,1)} copy(bf16[256,4096]{1,0:T(8,128)(2,1)S(1)} %hyena.1) | data formatting | bytes 4194304

commit v4 on v3

--- a/solution.py
+++ b/solution.py
@@ -14,6 +14,27 @@
 PAIR = 16
 MESH = pl.DeviceIdType.MESH
 F32 = jnp.float32
+
+
+SIDE = 4
+
+
+def hops(*steps):
+    return sum(min(step, SIDE - step) for step in steps)
+
+
+CHIPS = sorted(
+    [(dy, dx, dz) for dy in range(SIDE) for dx in range(SIDE) for dz in range(SIDE)][1:],
+    key=lambda steps: -hops(*steps),
+)
+NEAR = sorted(
+    [(dy, dz, dk) for dy in (0, SIDE // 2) for dz in range(SIDE) for dk in range(2)][1:],
+    key=lambda steps: -hops(*steps[:2]) - steps[2] / 2,
+)
+ACROSS = sorted(
+    [(dy, dx) for dy in range(2) for dx in range(SIDE)][1:],
+    key=lambda steps: -steps[0] - hops(steps[1]),
+)
 
 
 def token(t):
@@ -48,7 +69,6 @@
     head,
     power,
     power_block,
-    taps,
     state,
     got_state,
     before,
@@ -83,6 +103,43 @@
     mine = my_chan * n_seq + my_seq
     after = lax.rem(mine + 1, count)
     ahead = lax.rem(mine + count - 1, count)
+    chips = count // 2
+    my_chip = mine // 2
+    my_core = mine % 2
+    other = 1 - my_core
+    near = n_seq
+    across = n_chan
+    own = modes // near
+    my_near = my_seq
+    my_across = my_chan
+    plane = 2 * SIDE
+    my_z = my_seq % plane // 2
+    my_y = my_seq // plane * 2 + my_chan // SIDE
+    my_x = my_chan % SIDE
+    places_z = [lax.rem(my_z + d, SIDE) * 2 for d in range(SIDE)]
+    places_x = [lax.rem(my_x + d, SIDE) for d in range(SIDE)]
+    turned_y = [lax.rem(my_y + d, SIDE) for d in range(SIDE)]
+    chan_y = [y % 2 * SIDE for y in turned_y]
+    seq_y = [y // 2 * plane for y in turned_y]
+    cores = [my_core, other]
+    half_y = my_chan // SIDE
+    paired = [half_y * SIDE, (1 - half_y) * SIDE]
+
+    def device(dy=0, dx=0, dz=0, dk=0):
+        return (chan_y[dy] + places_x[dx], seq_y[dy] + places_z[dz] + cores[dk])
+
+    barrier = pltpu.get_barrier_semaphore()
+
+    def signal(target):
+        pl.semaphore_signal(barrier, inc=1, device_id=target, device_id_type=MESH)
+
+    for steps in CHIPS:
+        signal(device(*steps))
+    crossing = [(dy, dz) for dy, dz, dk in NEAR if dk]
+    for dy, dz in crossing:
+        signal(device(dy=dy, dz=dz, dk=1))
+    signal((ahead // n_seq, ahead % n_seq))
+    signals = len(CHIPS) + len(crossing) + 1
 
     def fetch(j, m):
         columns = pl.ds(m * WIDE, WIDE)
@@ -107,27 +164,6 @@
         for j in range(3):
             fetch(j, m).start()
 
-    chips = count // 2
-    my_chip = mine // 2
-    my_core = mine % 2
-    other = 1 - my_core
-
-    def device(chip, core):
-        per = n_seq // 2
-        return chip // per, chip % per * 2 + core
-
-    def signal(target):
-        pl.semaphore_signal(barrier, inc=1, device_id=target, device_id_type=MESH)
-
-    barrier = pltpu.get_barrier_semaphore()
-    for off in range(1, chips):
-        signal(device(lax.rem(my_chip + off, chips), my_core))
-    first_chip = my_chip - my_chip % (n_seq // 2)
-    for off in range(n_seq // 2):
-        signal(device(first_chip + off, other))
-    signal((ahead // n_seq, ahead % n_seq))
-    signals = chips - 1 + n_seq // 2 + 1
-
     for copy in small:
         copy.wait()
     for j in range(3):
@@ -144,36 +180,34 @@
         for b in range(quads):
             n = r * quads + b
             lanes = slice(b * part, (b + 1) * part)
-            params[my_chip, my_core, r : r + 1, lanes] = residues[n : n + 1, :] * jnp.sqrt(rates[n : n + 1, :])
-            params[my_chip, my_core, half + r : half + r + 1, lanes] = rates[n : n + 1, :]
-    params[my_chip, my_core, 2 * half : 2 * half + 1, 0:part] = direct[...]
-    params[my_chip, my_core, 2 * half : 2 * half + 1, part:] = jnp.zeros((1, LANES - part), F32)
-
-    used = pl.ds(0, 2 * half + 1)
-
-    def near_copy(off):
-        place = params.at[my_chip, my_core, used]
+            params[my_core, my_chip, r, :, lanes] = residues[n : n + 1, :] * jnp.sqrt(rates[n : n + 1, :])
+            params[my_core, my_chip, half + r, :, lanes] = rates[n : n + 1, :]
+    params[my_core, my_chip, 2 * half, :, 0:part] = direct[...]
+    params[my_core, my_chip, 2 * half, :, part:] = jnp.zeros((1, LANES - part), F32)
+
+    def near_copy(steps):
+        place = params.at[my_core, my_chip]
         return pltpu.make_async_remote_copy(
             src_ref=place,
             dst_ref=place,
             send_sem=send_near,
             recv_sem=recv_near,
-            device_id=device(lax.rem(my_chip + off, chips), my_core),
+            device_id=device(*steps),
             device_id_type=MESH,
         )
 
     def wait_near(sem):
-        some = params.at[pl.ds(0, chips - 1), 0, used]
+        some = params.at[0, pl.ds(0, chips - 1)]
         pltpu.make_async_copy(some, some, sem).wait()
 
     def far_copy(m):
-        place = params.at[pl.ds(m * (chips // groups), chips // groups), my_core, used]
+        place = params.at[my_core, pl.ds(m * (chips // groups), chips // groups)]
         return pltpu.make_async_remote_copy(
             src_ref=place,
             dst_ref=place,
             send_sem=send_far.at[m],
             recv_sem=recv_far.at[m],
-            device_id=device(my_chip, other),
+            device_id=device(dk=1),
             device_id_type=MESH,
         )
 
@@ -197,7 +231,7 @@
                 found.append(
                     jnp.concatenate(
                         [
-                            params[((m * ROWS + j) * quads + i) // 2, i % 2, row : row + 1, :]
+                            params[i % 2, ((m * ROWS + j) * quads + i) // 2, row, :, :]
                             for j in range(ROWS)
                         ],
                         axis=0,
@@ -285,57 +319,69 @@
                 head[m, 2 * j + t] = tiles[j, token(t), :]
 
     def gather_states(m):
-        def step(b, states):
-            values = [
-                gated[m, pl.ds(pl.multiple_of((b * BLOCK + i) * ROWS, ROWS), ROWS), :]
-                for i in range(BLOCK)
-            ]
-            results = []
-            for n in range(modes):
-                rate = power[n, m]
-                end = values[0]
-                for i in range(1, BLOCK):
-                    end = rate * end + values[i]
-                end = weight[n, m] * end
-                ends[m, b, n] = end
-                results.append(power_block[n, m] * states[n] + end)
-            return tuple(results)
-
-        zero = jnp.zeros((ROWS, LANES), F32)
-        states = lax.fori_loop(0, length // BLOCK, step, (zero,) * modes)
-        for n in range(modes):
-            state[m, n] = states[n]
-
-    def state_copy(m, off):
-        peer = lax.rem(my_seq + off, n_seq)
+        some = modes // 2
+        for part in range(0, modes, some):
+            chosen = range(part, part + some)
+            rate = [power[n, m] for n in chosen]
+            rate_block = [power_block[n, m] for n in chosen]
+            heavy = [weight[n, m] for n in chosen]
+
+            def step(pair, states):
+                for half in range(PAIR // BLOCK):
+                    b = pair * (PAIR // BLOCK) + half
+                    values = [
+                        gated[m, pl.ds(pl.multiple_of((b * BLOCK + i) * ROWS, ROWS), ROWS), :]
+                        for i in range(BLOCK)
+                    ]
+                    results = []
+                    for k, n in enumerate(chosen):
+                        end = values[0]
+                        for i in range(1, BLOCK):
+                            end = rate[k] * end + values[i]
+                        end = heavy[k] * end
+                        ends[m, b, n] = end
+                        results.append(rate_block[k] * states[k] + end)
+                    states = tuple(results)
+                return states
+
+            zero = jnp.zeros((ROWS, LANES), F32)
+            states = lax.fori_loop(0, length // PAIR, step, (zero,) * some)
+            for k, n in enumerate(chosen):
+                state[m, n // own, n % own] = states[k]
+
+    def state_copy(m, steps):
+        dy, dz, dk = steps
+        target = device(dy=dy, dz=dz, dk=dk)
+        peer = target[1]
         return pltpu.make_async_remote_copy(
             src_ref=state.at[m, peer],
-            dst_ref=got_state.at[m, my_seq],
+            dst_ref=got_state.at[m, my_near],
             send_sem=send_state.at[m],
             recv_sem=recv_state.at[m],
-            device_id=(my_chan, peer),
+            device_id=target,
             device_id_type=MESH,
         )
 
-    def total_copy(m, off):
-        peer = lax.rem(my_chan + off, n_chan)
+    def total_copy(m, steps):
         return pltpu.make_async_remote_copy(
             src_ref=total.at[m],
-            dst_ref=got_total.at[m, my_chan],
+            dst_ref=got_total.at[m, my_across],
             send_sem=send_total.at[m],
             recv_sem=recv_total.at[m],
-            device_id=(peer, my_seq),
+            device_id=(paired[steps[0]] + places_x[steps[1]], my_seq),
             device_id_type=MESH,
         )
 
-    def back_copy(m, off):
-        peer = lax.rem(my_seq + off, n_seq)
+    def back_copy(m, steps):
+        dy, dz, dk = steps
+        target = device(dy=dy, dz=dz, dk=dk)
+        peer = target[1]
         return pltpu.make_async_remote_copy(
             src_ref=back.at[m, peer],
-            dst_ref=carried.at[m, my_seq],
+            dst_ref=carried.at[m, my_near],
             send_sem=send_back.at[m],
             recv_sem=recv_back.at[m],
-            device_id=(my_chan, peer),
+            device_id=target,
             device_id_type=MESH,
         )
 
@@ -344,64 +390,79 @@
         pltpu.make_async_copy(some, some, sem.at[m]).wait()
 
     def send_states(m):
-        for off in range(1, n_seq):
-            state_copy(m, off).start()
-        got_state[m, my_seq] = state[m, my_seq]
+        for steps in NEAR:
+            state_copy(m, steps).start()
+        got_state[m, my_near] = state[m, my_near]
 
     def scan_group(m):
-        wait_bytes(got_state, n_seq - 1, m, recv_state)
-        shrink = jnp.exp(-float(length) * decay[my_seq, m])
-        running = jnp.zeros((ROWS, LANES), F32)
-        for k in range(n_seq):
-            before[m, k] = running
-            running = shrink * running + got_state[m, k]
-        total[m] = running
-        for off in range(1, n_chan):
-            total_copy(m, off).start()
+        wait_bytes(got_state, near - 1, m, recv_state)
+        for u in range(own):
+            shrink = jnp.exp(-float(length) * decay[my_near * own + u, m])
+            running = jnp.zeros((ROWS, LANES), F32)
+            for k in range(near):
+                before[m, k, u] = running
+                running = shrink * running + got_state[m, k, u]
+            total[m, u] = running
+        for steps in ACROSS:
+            total_copy(m, steps).start()
 
     def scan_all(m):
-        wait_bytes(got_total, n_chan - 1, m, recv_total)
-        rate = decay[my_seq, m]
-        shrink = jnp.exp(-float(length) * rate)
-        shrink_group = jnp.exp(-float(length * n_seq) * rate)
-        running = jnp.zeros((ROWS, LANES), F32)
-        for c in range(n_chan - 1):
-            running = jnp.where(c < my_chan, shrink_group * running + got_total[m, c], running)
-        for k in range(n_seq):
-            back[m, k] = before[m, k] + running
-            running = shrink * running
-        for off in range(1, n_seq):
-            back_copy(m, off).start()
-        carried[m, my_seq] = back[m, my_seq]
+        wait_bytes(got_total, across - 1, m, recv_total)
+        for u in range(own):
+            rate = decay[my_near * own + u, m]
+            shrink = jnp.exp(-float(length) * rate)
+            shrink_group = jnp.exp(-float(length * near) * rate)
+            running = jnp.zeros((ROWS, LANES), F32)
+            for c in range(across - 1):
+                running = jnp.where(
+                    c < my_across, shrink_group * running + got_total[m, c, u], running
+                )
+            for k in range(near):
+                back[m, k, u] = before[m, k, u] + running
+                running = shrink * running
+        for steps in NEAR:
+            back_copy(m, steps).start()
+        carried[m, my_near] = back[m, my_near]
 
     def write(m):
         columns = pl.ds(m * WIDE, WIDE)
         return pltpu.make_async_copy(out_rows.at[:, columns], out_hbm.at[:, columns], out_sem.at[m])
 
-    def convolve(m):
-        wait_bytes(carried, n_seq - 1, m, recv_back)
+    def block_places(b):
+        return [pl.ds(pl.multiple_of((b * BLOCK + i) * ROWS, ROWS), ROWS) for i in range(BLOCK)]
+
+    def convolve_block(m):
         term = [weight[n, m] for n in range(modes)]
+        taps = []
         for i in range(BLOCK):
             tap = term[0]
             for n in range(1, modes):
                 tap = tap + term[n]
-            taps[i] = tap + skip[m] if i == 0 else tap
+            taps.append(tap + skip[m] if i == 0 else tap)
             if i < BLOCK - 1:
                 term = [term[n] * power[n, m] for n in range(modes)]
 
-        def step(pair, states):
+        def step(pair, _):
             for half in range(PAIR // BLOCK):
-                b = pair * (PAIR // BLOCK) + half
-                places = [
-                    pl.ds(pl.multiple_of((b * BLOCK + i) * ROWS, ROWS), ROWS) for i in range(BLOCK)
-                ]
+                places = block_places(pair * (PAIR // BLOCK) + half)
                 values = [gated[m, places[i], :] for i in range(BLOCK)]
-                sums = []
                 for i in range(BLOCK):
                     one = taps[0] * values[i]
                     for j in range(1, i + 1):
                         one = one + taps[j] * values[i - j]
-                    sums.append(one)
+                    gated[m, places[i], :] = one
+            return 0
+
+        lax.fori_loop(0, length // PAIR, step, 0)
+
+    def convolve(m):
+        wait_bytes(carried, near - 1, m, recv_back)
+
+        def step(pair, states):
+            for half in range(PAIR // BLOCK):
+                b = pair * (PAIR // BLOCK) + half
+                places = block_places(b)
+                sums = [gated[m, places[i], :] for i in range(BLOCK)]
                 results = []
                 for n in range(modes):
                     rate = power[n, m]
@@ -424,39 +485,38 @@
                 )
             return states
 
-        lax.fori_loop(0, length // PAIR, step, tuple(carried[m, n] for n in range(modes)))
+        lax.fori_loop(0, length // PAIR, step, tuple(carried[m, n // own, n % own] for n in range(modes)))
         write(m).start()
 
     pl.semaphore_wait(barrier, signals)
-    for off in range(1, chips):
-        near_copy(off).start()
+    for steps in CHIPS:
+        near_copy(steps).start()
     for m in range(groups):
         feature(m)
     wait_near(recv_near)
     for m in range(groups):
         far_copy(m).start()
-    for m in range(groups):
+    def first(m):
         patch(m)
         spread_params(m)
         gather_states(m)
         send_states(m)
-    scan_group(0)
-    for m in range(1, groups):
-        scan_group(m)
-        if m >= 2:
-            scan_all(m - 2)
-    scan_all(groups - 2)
-    scan_all(groups - 1)
-    for m in range(groups):
-        convolve(m)
+
+    steps = [(first, 0), (first, 1), (first, 2), (first, 3)]
+    steps += [(scan_group, 0), (convolve_block, 0), (scan_group, 1), (convolve_block, 1)]
+    steps += [(scan_group, 2), (convolve_block, 2), (scan_all, 0), (scan_group, 3)]
+    steps += [(convolve_block, 3), (scan_all, 1), (scan_all, 2), (scan_all, 3)]
+    steps += [(convolve, 0), (convolve, 1), (convolve, 2), (convolve, 3)]
+    for act, m in steps:
+        act(m)
     wait_near(send_near)
     for m in range(groups):
         write(m).wait()
         halo_copy(m).wait_send()
         far_copy(m).wait_send()
-        wait_bytes(got_state, n_seq - 1, m, send_state)
-        wait_bytes(got_total, n_chan - 1, m, send_total)
-        wait_bytes(carried, n_seq - 1, m, send_back)
+        wait_bytes(got_state, near - 1, m, send_state)
+        wait_bytes(got_total, across - 1, m, send_total)
+        wait_bytes(carried, near - 1, m, send_back)
 
 
 def shards(n_chan, n_seq, projected, short_filter, residues, decays, skip):
@@ -466,6 +526,9 @@
     hbm = pl.BlockSpec(memory_space=pltpu.HBM)
     dma = pltpu.SemaphoreType.DMA
     blocks = length // BLOCK
+    near = n_seq
+    own = modes // near
+    rows = 2 * modes * residues.shape[1] // LANES + 1
     return pl.pallas_call(
         functools.partial(kernel, n_chan, n_seq),
         out_shape=jax.ShapeDtypeStruct((length, width), projected.dtype),
@@ -482,7 +545,7 @@
             pltpu.VMEM((groups, length * ROWS, LANES), F32),
             pltpu.VMEM((groups, length * ROWS, LANES), F32),
             pltpu.VMEM((groups, blocks, modes, ROWS, LANES), F32),
-            pltpu.VMEM((n_chan * n_seq // 2, 2, 2 * ROWS, LANES), F32),
+            pltpu.VMEM((2, n_chan * n_seq // 2, rows, 1, LANES), F32),
             pltpu.VMEM((modes, groups, ROWS, LANES), F32),
             pltpu.VMEM((modes, groups, ROWS, LANES), F32),
             pltpu.VMEM((groups, ROWS, LANES), F32),
@@ -491,14 +554,13 @@
             pltpu.VMEM((groups, 6, ROWS, LANES), F32),
             pltpu.VMEM((modes, groups, ROWS, LANES), F32),
             pltpu.VMEM((modes, groups, ROWS, LANES), F32),
-            pltpu.VMEM((BLOCK, ROWS, LANES), F32),
-            pltpu.VMEM((groups, modes, ROWS, LANES), F32),
-            pltpu.VMEM((groups, n_seq, ROWS, LANES), F32),
-            pltpu.VMEM((groups, n_seq, ROWS, LANES), F32),
-            pltpu.VMEM((groups, ROWS, LANES), F32),
-            pltpu.VMEM((groups, n_chan, ROWS, LANES), F32),
-            pltpu.VMEM((groups, n_seq, ROWS, LANES), F32),
-            pltpu.VMEM((groups, modes, ROWS, LANES), F32),
+            pltpu.VMEM((groups, near, own, ROWS, LANES), F32),
+            pltpu.VMEM((groups, near, own, ROWS, LANES), F32),
+            pltpu.VMEM((groups, near, own, ROWS, LANES), F32),
+            pltpu.VMEM((groups, own, ROWS, LANES), F32),
+            pltpu.VMEM((groups, n_chan * n_seq // near, own, ROWS, LANES), F32),
+            pltpu.VMEM((groups, near, own, ROWS, LANES), F32),
+            pltpu.VMEM((groups, near, own, ROWS, LANES), F32),
             pltpu.VMEM((PAIR * ROWS, LANES), F32),
             pltpu.VMEM((length, width), projected.dtype),
             dma((groups, 3)),

time: 44.9 us -> 40.5 us (0.902)
  Pallas kernels: 43.5 us -> 39 us
    pallas_call x1, Pallas kernels: 43.5 us -> 39 us  [shards(): pl.pallas_call(functools.partial(kernel, n_chan, n_seq), out_shape=jax.Sh...]
where the time goes in v4:
time: 40.5 us; the launch traced here: 40.4 us
  Pallas kernels  39 us (96%)
  local copies, waits for them, and re-layouts  1.32 us (3%)
    pallas_call x1, Pallas kernels, shards(): pl.pallas_call(functools.partial(kernel, n_chan, n_seq), out_shape=jax.Sh...  39 us
    unnamed x1, local copies, waits for them, and re-layouts  1.32 us

profile of v4, /device:TPU:1, one launch (start us, length us, event | category | flops | bytes accessed | tf_op | source)
XLA Modules:
  0.0 40.4 jit_solution(9288168408218149523)
XLA Ops:
  0.0 39.0 %hyena.1 = bf16[256,4096]{1,0:T(8,128)(2,1)S(1)} custom-call(bf16[3,256,4096]{2,1,0:T(8,128)(2,1)} %x_hbm.1, f32[3,3,4096]{2,1,0:T(4,128)} %filt_hbm.1, f32[16,32]{1,0:T(8,128)} %residues_hbm.1, f32[16,32]{1,0:T(8,128)} %rates_hbm.1, f32[1,32]{1,0:T(1,128)} %bitcast.1), custom_call_target="tpu_custom_call" | custom-call | tf_op jit(solution)/shard_map/hyena/pallas_call | solution.py:532
  39.0 1.3 %copy.7 = bf16[256,4096]{1,0:T(8,128)(2,1)} copy(bf16[256,4096]{1,0:T(8,128)(2,1)S(1)} %hyena.1) | data formatting | bytes 4194304

commit v5 on v4

--- a/solution.py
+++ b/solution.py
@@ -28,12 +28,11 @@
     key=lambda steps: -hops(*steps),
 )
 NEAR = sorted(
-    [(dy, dz, dk) for dy in (0, SIDE // 2) for dz in range(SIDE) for dk in range(2)][1:],
-    key=lambda steps: -hops(*steps[:2]) - steps[2] / 2,
+    [(dz, dk) for dz in range(SIDE) for dk in range(2)][1:],
+    key=lambda steps: -hops(steps[0]) - steps[1] / 2,
 )
 ACROSS = sorted(
-    [(dy, dx) for dy in range(2) for dx in range(SIDE)][1:],
-    key=lambda steps: -steps[0] - hops(steps[1]),
+    [(dy, dx) for dy in range(SIDE) for dx in range(SIDE)][1:], key=lambda steps: -hops(*steps)
 )
 
 
@@ -107,11 +106,11 @@
     my_chip = mine // 2
     my_core = mine % 2
     other = 1 - my_core
-    near = n_seq
-    across = n_chan
+    near = 2 * SIDE
+    across = count // near
     own = modes // near
-    my_near = my_seq
-    my_across = my_chan
+    my_near = mine % near
+    my_across = mine // near
     plane = 2 * SIDE
     my_z = my_seq % plane // 2
     my_y = my_seq // plane * 2 + my_chan // SIDE
@@ -122,8 +121,6 @@
     chan_y = [y % 2 * SIDE for y in turned_y]
     seq_y = [y // 2 * plane for y in turned_y]
     cores = [my_core, other]
-    half_y = my_chan // SIDE
-    paired = [half_y * SIDE, (1 - half_y) * SIDE]
 
     def device(dy=0, dx=0, dz=0, dk=0):
         return (chan_y[dy] + places_x[dx], seq_y[dy] + places_z[dz] + cores[dk])
@@ -135,9 +132,9 @@
 
     for steps in CHIPS:
         signal(device(*steps))
-    crossing = [(dy, dz) for dy, dz, dk in NEAR if dk]
-    for dy, dz in crossing:
-        signal(device(dy=dy, dz=dz, dk=1))
+    crossing = [dz for dz, dk in NEAR if dk]
+    for dz in crossing:
+        signal(device(dz=dz, dk=1))
     signal((ahead // n_seq, ahead % n_seq))
     signals = len(CHIPS) + len(crossing) + 1
 
@@ -350,9 +347,9 @@
                 state[m, n // own, n % own] = states[k]
 
     def state_copy(m, steps):
-        dy, dz, dk = steps
-        target = device(dy=dy, dz=dz, dk=dk)
-        peer = target[1]
+        dz, dk = steps
+        target = device(dz=dz, dk=dk)
+        peer = target[1] % near
         return pltpu.make_async_remote_copy(
             src_ref=state.at[m, peer],
             dst_ref=got_state.at[m, my_near],
@@ -362,20 +359,26 @@
             device_id_type=MESH,
         )
 
-    def total_copy(m, steps):
-        return pltpu.make_async_remote_copy(
-            src_ref=total.at[m],
-            dst_ref=got_total.at[m, my_across],
-            send_sem=send_total.at[m],
-            recv_sem=recv_total.at[m],
-            device_id=(paired[steps[0]] + places_x[steps[1]], my_seq),
-            device_id_type=MESH,
-        )
+    def each_total(m, act):
+        for i, steps in enumerate(ACROSS):
+            target = device(*steps)
+            copy = pltpu.make_async_remote_copy(
+                src_ref=total.at[m],
+                dst_ref=got_total.at[m, my_across],
+                send_sem=send_total.at[m, i],
+                recv_sem=recv_total.at[m, my_across],
+                device_id=target,
+                device_id_type=MESH,
+            )
+
+            @pl.when(target[0] * 2 + target[1] // near > my_across)
+            def _():
+                act(copy)
 
     def back_copy(m, steps):
-        dy, dz, dk = steps
-        target = device(dy=dy, dz=dz, dk=dk)
-        peer = target[1]
+        dz, dk = steps
+        target = device(dz=dz, dk=dk)
+        peer = target[1] % near
         return pltpu.make_async_remote_copy(
             src_ref=back.at[m, peer],
             dst_ref=carried.at[m, my_near],
@@ -403,11 +406,17 @@
                 before[m, k, u] = running
                 running = shrink * running + got_state[m, k, u]
             total[m, u] = running
-        for steps in ACROSS:
-            total_copy(m, steps).start()
+        each_total(m, lambda copy: copy.start())
 
     def scan_all(m):
-        wait_bytes(got_total, across - 1, m, recv_total)
+        for c in range(across - 1):
+            place = got_total.at[m, c]
+            arrival = pltpu.make_async_copy(place, place, recv_total.at[m, c])
+
+            @pl.when(c < my_across)
+            def _():
+                arrival.wait()
+
         for u in range(own):
             rate = decay[my_near * own + u, m]
             shrink = jnp.exp(-float(length) * rate)
@@ -502,10 +511,10 @@
         gather_states(m)
         send_states(m)
 
-    steps = [(first, 0), (first, 1), (first, 2), (first, 3)]
-    steps += [(scan_group, 0), (convolve_block, 0), (scan_group, 1), (convolve_block, 1)]
-    steps += [(scan_group, 2), (convolve_block, 2), (scan_all, 0), (scan_group, 3)]
-    steps += [(convolve_block, 3), (scan_all, 1), (scan_all, 2), (scan_all, 3)]
+    steps = [(first, 0), (first, 1), (first, 2), (scan_group, 0), (first, 3)]
+    steps += [(scan_group, 1), (convolve_block, 0), (scan_group, 2), (convolve_block, 1)]
+    steps += [(scan_all, 0), (scan_group, 3), (convolve_block, 2), (scan_all, 1)]
+    steps += [(convolve_block, 3), (scan_all, 2), (scan_all, 3)]
     steps += [(convolve, 0), (convolve, 1), (convolve, 2), (convolve, 3)]
     for act, m in steps:
         act(m)
@@ -515,7 +524,7 @@
         halo_copy(m).wait_send()
         far_copy(m).wait_send()
         wait_bytes(got_state, near - 1, m, send_state)
-        wait_bytes(got_total, across - 1, m, send_total)
+        each_total(m, lambda copy: copy.wait_send())
         wait_bytes(carried, near - 1, m, send_back)
 
 
@@ -526,7 +535,8 @@
     hbm = pl.BlockSpec(memory_space=pltpu.HBM)
     dma = pltpu.SemaphoreType.DMA
     blocks = length // BLOCK
-    near = n_seq
+    near = 2 * SIDE
+    across = n_chan * n_seq // near
     own = modes // near
     rows = 2 * modes * residues.shape[1] // LANES + 1
     return pl.pallas_call(
@@ -558,7 +568,7 @@
             pltpu.VMEM((groups, near, own, ROWS, LANES), F32),
             pltpu.VMEM((groups, near, own, ROWS, LANES), F32),
             pltpu.VMEM((groups, own, ROWS, LANES), F32),
-            pltpu.VMEM((groups, n_chan * n_seq // near, own, ROWS, LANES), F32),
+            pltpu.VMEM((groups, across, own, ROWS, LANES), F32),
             pltpu.VMEM((groups, near, own, ROWS, LANES), F32),
             pltpu.VMEM((groups, near, own, ROWS, LANES), F32),
             pltpu.VMEM((PAIR * ROWS, LANES), F32),
@@ -574,8 +584,8 @@
             dma((groups,)),
             dma((groups,)),
             dma((groups,)),
-            dma((groups,)),
-            dma((groups,)),
+            dma((groups, across - 1)),
+            dma((groups, across)),
             dma((groups,)),
             dma((groups,)),
         ],

time: 40.5 us -> 38.9 us (0.960)
  Pallas kernels: 39 us -> 37.5 us
    pallas_call x1, Pallas kernels: 39 us -> 37.5 us  [shards(): pl.pallas_call(functools.partial(kernel, n_chan, n_seq), out_shape=jax.Sh...]
where the time goes in v5:
time: 38.9 us; the launch traced here: 38.8 us
  Pallas kernels  37.5 us (96%)
  local copies, waits for them, and re-layouts  1.32 us (3%)
    pallas_call x1, Pallas kernels, shards(): pl.pallas_call(functools.partial(kernel, n_chan, n_seq), out_shape=jax.Sh...  37.5 us
    unnamed x1, local copies, waits for them, and re-layouts  1.32 us

profile of v5, /device:TPU:1, one launch (start us, length us, event | category | flops | bytes accessed | tf_op | source)
XLA Modules:
  0.0 38.8 jit_solution(12250757225946131726)
XLA Ops:
  0.0 37.5 %hyena.1 = bf16[256,4096]{1,0:T(8,128)(2,1)S(1)} custom-call(bf16[3,256,4096]{2,1,0:T(8,128)(2,1)} %x_hbm.1, f32[3,3,4096]{2,1,0:T(4,128)} %filt_hbm.1, f32[16,32]{1,0:T(8,128)} %residues_hbm.1, f32[16,32]{1,0:T(8,128)} %rates_hbm.1, f32[1,32]{1,0:T(1,128)} %bitcast.1), custom_call_target="tpu_custom_call" | custom-call | tf_op jit(solution)/shard_map/hyena/pallas_call | solution.py:542
  37.5 1.3 %copy.7 = bf16[256,4096]{1,0:T(8,128)(2,1)} copy(bf16[256,4096]{1,0:T(8,128)(2,1)S(1)} %hyena.1) | data formatting | bytes 4194304

commit v6 on v5

--- a/solution.py
+++ b/solution.py
@@ -12,6 +12,7 @@
 WIDE = LANES * ROWS
 BLOCK = 8
 PAIR = 16
+PIECES = 2
 MESH = pl.DeviceIdType.MESH
 F32 = jnp.float32
 
@@ -433,9 +434,12 @@
             back_copy(m, steps).start()
         carried[m, my_near] = back[m, my_near]
 
-    def write(m):
+    def write(m, piece):
         columns = pl.ds(m * WIDE, WIDE)
-        return pltpu.make_async_copy(out_rows.at[:, columns], out_hbm.at[:, columns], out_sem.at[m])
+        rows = pl.ds(piece * (length // PIECES), length // PIECES)
+        return pltpu.make_async_copy(
+            out_rows.at[rows, columns], out_hbm.at[rows, columns], out_sem.at[m, piece]
+        )
 
     def block_places(b):
         return [pl.ds(pl.multiple_of((b * BLOCK + i) * ROWS, ROWS), ROWS) for i in range(BLOCK)]
@@ -494,8 +498,11 @@
                 )
             return states
 
-        lax.fori_loop(0, length // PAIR, step, tuple(carried[m, n // own, n % own] for n in range(modes)))
-        write(m).start()
+        states = tuple(carried[m, n // own, n % own] for n in range(modes))
+        steps = length // PAIR // PIECES
+        for piece in range(PIECES):
+            states = lax.fori_loop(piece * steps, (piece + 1) * steps, step, states)
+            write(m, piece).start()
 
     pl.semaphore_wait(barrier, signals)
     for steps in CHIPS:
@@ -520,7 +527,8 @@
         act(m)
     wait_near(send_near)
     for m in range(groups):
-        write(m).wait()
+        for piece in range(PIECES):
+            write(m, piece).wait()
         halo_copy(m).wait_send()
         far_copy(m).wait_send()
         wait_bytes(got_state, near - 1, m, send_state)
@@ -575,7 +583,7 @@
             pltpu.VMEM((length, width), projected.dtype),
             dma((groups, 3)),
             dma((4,)),
-            dma((groups,)),
+            dma((groups, PIECES)),
             dma,
             dma,
             dma((groups,)),

time: 38.9 us -> 39 us (level)
  no operation moved by 1% of the time
where the time goes in v6:
time: 39 us; the launch traced here: 38.9 us
  Pallas kernels  37.6 us (96%)
  local copies, waits for them, and re-layouts  1.32 us (3%)
    pallas_call x1, Pallas kernels, shards(): pl.pallas_call(functools.partial(kernel, n_chan, n_seq), out_shape=jax.Sh...  37.6 us
    unnamed x1, local copies, waits for them, and re-layouts  1.32 us

profile of v6, /device:TPU:1, one launch (start us, length us, event | category | flops | bytes accessed | tf_op | source)
XLA Modules:
  0.0 38.9 jit_solution(8044118519344235412)
XLA Ops:
  0.0 37.6 %hyena.1 = bf16[256,4096]{1,0:T(8,128)(2,1)S(1)} custom-call(bf16[3,256,4096]{2,1,0:T(8,128)(2,1)} %x_hbm.1, f32[3,3,4096]{2,1,0:T(4,128)} %filt_hbm.1, f32[16,32]{1,0:T(8,128)} %residues_hbm.1, f32[16,32]{1,0:T(8,128)} %rates_hbm.1, f32[1,32]{1,0:T(1,128)} %bitcast.1), custom_call_target="tpu_custom_call" | custom-call | tf_op jit(solution)/shard_map/hyena/pallas_call | solution.py:550
  37.6 1.3 %copy.7 = bf16[256,4096]{1,0:T(8,128)(2,1)} copy(bf16[256,4096]{1,0:T(8,128)(2,1)S(1)} %hyena.1) | data formatting | bytes 4194304

commit v7 on v6

--- a/solution.py
+++ b/solution.py
@@ -520,8 +520,8 @@
 
     steps = [(first, 0), (first, 1), (first, 2), (scan_group, 0), (first, 3)]
     steps += [(scan_group, 1), (convolve_block, 0), (scan_group, 2), (convolve_block, 1)]
-    steps += [(scan_all, 0), (scan_group, 3), (convolve_block, 2), (scan_all, 1)]
-    steps += [(convolve_block, 3), (scan_all, 2), (scan_all, 3)]
+    steps += [(scan_all, 0), (scan_group, 3), (scan_all, 1), (convolve_block, 2)]
+    steps += [(scan_all, 2), (convolve_block, 3), (scan_all, 3)]
     steps += [(convolve, 0), (convolve, 1), (convolve, 2), (convolve, 3)]
     for act, m in steps:
         act(m)

time: 39 us -> 39 us (level); the launches traced: 38.9 us -> 38.2 us
  Pallas kernels: 37.6 us -> 36.9 us
    pallas_call x1, Pallas kernels: 37.6 us -> 36.9 us  [shards(): pl.pallas_call(functools.partial(kernel, n_chan, n_seq), out_shape=jax.Sh...]
where the time goes in v7:
time: 39 us; the launch traced here: 38.2 us
  Pallas kernels  36.9 us (95%)
  local copies, waits for them, and re-layouts  1.32 us (3%)
    pallas_call x1, Pallas kernels, shards(): pl.pallas_call(functools.partial(kernel, n_chan, n_seq), out_shape=jax.Sh...  36.9 us
    unnamed x1, local copies, waits for them, and re-layouts  1.32 us

profile of v7, /device:TPU:1, one launch (start us, length us, event | category | flops | bytes accessed | tf_op | source)
XLA Modules:
  0.0 38.2 jit_solution(11676271421097330814)
XLA Ops:
  0.0 36.9 %hyena.1 = bf16[256,4096]{1,0:T(8,128)(2,1)S(1)} custom-call(bf16[3,256,4096]{2,1,0:T(8,128)(2,1)} %x_hbm.1, f32[3,3,4096]{2,1,0:T(4,128)} %filt_hbm.1, f32[16,32]{1,0:T(8,128)} %residues_hbm.1, f32[16,32]{1,0:T(8,128)} %rates_hbm.1, f32[1,32]{1,0:T(1,128)} %bitcast.1), custom_call_target="tpu_custom_call" | custom-call | tf_op jit(solution)/shard_map/hyena/pallas_call | solution.py:550
  36.9 1.3 %copy.7 = bf16[256,4096]{1,0:T(8,128)(2,1)} copy(bf16[256,4096]{1,0:T(8,128)(2,1)S(1)} %hyena.1) | data formatting | bytes 4194304
